TPU v7x, 256 devices: a whole 4x4x8 slice. The times are simulated.
256 devices in a mesh: inst: 32 (over z, y), tensor: 8 (over x, core).
Axes of the slice: x: 4, y: 4, z: 8, core: 2. Of those that a mesh axis runs over, the one named last changes fastest.
Arguments:
- queries: bfloat16 [32, 4, 8192], P('inst', None, 'tensor'), may hold values from -6 to 6
- new_states: bfloat16 [32, 4, 8192], P('inst', None, 'tensor'), may hold values from -24 to 24
- key_weight: bfloat16 [8192, 1024], P(None, 'tensor'), may hold values from -0.0625 to 0.0625
- value_weight: bfloat16 [8192, 1024], P(None, 'tensor'), may hold values from -0.0625 to 0.0625
- key_pool: bfloat16 [2048, 256, 1024], P('inst', None, 'tensor'), may hold values from -512 to 512
- value_pool: bfloat16 [2048, 256, 1024], P('inst', None, 'tensor'), may hold values from -6 to 6
- lengths: int32 [32], replicated, may hold values from 2048 to 16384, as said below
- page_table: int32 [32, 64], replicated, may hold values from -1 to 2047, as said below
Outputs:
- attention: bfloat16 [32, 4, 8192], P('inst', None, 'tensor')
Inputs may be any that keep to these rules, and one draw needn't show every extreme that they name: `lengths`: half of the requests have at most 8192 tokens and the others more; one request has exactly 16384. `page_table`: entry [r, j] is the pool slot (instance index times 64 plus a slot of that instance) of page j of request r for j < ceil(lengths[r] / 256), and -1 beyond; no slot is named twice. Request r is served by instance r; a request of at most 8192 tokens has all its pages there; each longer request of n pages has n // 4 consecutive pages on one other instance, which serves a request of at most 8192 tokens, and the rest on instance r; an instance holds lent pages of at most one request. Some request lends to the instance 32 // 2 indices away and some request lends to the instance one index below it.
All inputs are finite; a program needn't handle non-finite values.
Results may differ from a plain program's by a relative error of at most 0.0072.
Values may be sent and summed in bfloat16 or wider, within the bound.
A program may use at most 128 MiB of HBM per device.

v0:
```python
import math

import jax
import jax.numpy as jnp
from jax import lax
from jax.sharding import PartitionSpec as P

HD = 128


negative_fill = -1e30


def combined_all(value, axis, join):
    pieces = jax.tree.map(lambda part: lax.all_gather(part, axis), value)
    head = jax.tree.map(lambda part: part[0], pieces)
    tail = jax.tree.map(lambda part: part[1:], pieces)
    subtotal, _ = lax.scan(lambda subtotal, slab: (join(subtotal, slab), None), head, tail)
    return subtotal


def join_parts(this_part, other_part):
    highest = jnp.maximum(this_part[0], other_part[0])
    this_scale = jnp.exp(this_part[0] - highest)
    other_scale = jnp.exp(other_part[0] - highest)
    weight_total = this_part[1] * this_scale + other_part[1] * other_scale
    numerator = this_part[2] * this_scale[..., None] + other_part[2] * other_scale[..., None]
    return (highest, weight_total, numerator)


def on_device(
    queries, new_states, key_weight, value_weight, key_pool, value_pool, lengths, page_table
):
    req_dev, step_count, query_cols = queries.shape
    slot_count, page_len, kv_cols = key_pool.shape
    request_count, page_max_count = page_table.shape
    kv_dev = kv_cols // HD
    group_size = query_cols // kv_cols
    score_scale = 1.0 / math.sqrt(HD)
    state_rows = new_states.reshape(req_dev * step_count, new_states.shape[2])
    shard_piece = lax.all_gather(state_rows, "tensor", axis=1, tiled=True)
    key_sum = jnp.dot(shard_piece, key_weight, preferred_element_type=jnp.float32)
    value_sum = jnp.dot(shard_piece, value_weight, preferred_element_type=jnp.float32)
    new_keys = key_sum.astype(jnp.bfloat16).reshape(req_dev, step_count, kv_dev, HD)
    new_values = value_sum.astype(jnp.bfloat16).reshape(req_dev, step_count, kv_dev, HD)
    every_query = lax.all_gather(queries, "inst", axis=0, tiled=True)
    slot_base = lax.axis_index("inst") * slot_count
    global_ids = slot_base + jnp.arange(slot_count, dtype=jnp.int32)
    matches = (page_table[None, :, :] == global_ids[:, None, None]).astype(jnp.int32)
    owner_hot = jnp.sum(matches, axis=2)
    page_number = jnp.sum(
        matches * jnp.arange(page_max_count, dtype=jnp.int32)[None, None, :], axis=(1, 2)
    )
    owners = jnp.sum(owner_hot * jnp.arange(request_count, dtype=jnp.int32)[None, :], axis=1)
    limits = jnp.sum(owner_hot * lengths[None, :], axis=1)
    positions = page_number[:, None] * page_len + jnp.arange(page_len, dtype=jnp.int32)[None, :]
    valid_mask = (positions < limits[:, None])[:, None, None, None, :]
    page_queries = jnp.take(every_query, owners, axis=0).reshape(
        slot_count, step_count, kv_dev, group_size, HD
    )
    page_keys = key_pool.reshape(slot_count, page_len, kv_dev, HD)
    page_values = value_pool.reshape(slot_count, page_len, kv_dev, HD)
    scores = (
        jnp.einsum("bskgd,bpkd->bkgsp", page_queries, page_keys, preferred_element_type=jnp.float32)
        * score_scale
    )
    masked = jnp.where(valid_mask, scores, negative_fill)
    page_highest = masked.max(axis=4)
    owner_flag = (owner_hot > 0)[:, :, None, None, None]
    request_highest = jnp.max(jnp.where(owner_flag, page_highest[:, None], negative_fill), axis=0)
    slot_highest = jnp.take(request_highest, owners, axis=0)
    weights = jnp.where(valid_mask, jnp.exp(masked - slot_highest[..., None]), 0.0)
    owner_float = owner_hot.astype(jnp.float32)
    request_total = jnp.einsum(
        "br,bkgs->rkgs", owner_float, weights.sum(axis=4), precision=lax.Precision.HIGHEST
    )
    page_out = jnp.einsum(
        "bkgsp,bpkd->bkgsd",
        weights.astype(jnp.bfloat16),
        page_values,
        preferred_element_type=jnp.float32,
    )
    request_out = jnp.einsum(
        "br,bkgsd->rkgsd", owner_float, page_out, precision=lax.Precision.HIGHEST
    )
    all_highest, all_total, all_out = combined_all(
        (request_highest, request_total, request_out), "inst", join_parts
    )
    row_start = lax.axis_index("inst") * req_dev
    remote_highest = lax.dynamic_slice_in_dim(all_highest, row_start, req_dev, 0)
    remote_total = lax.dynamic_slice_in_dim(all_total, row_start, req_dev, 0)
    remote_out = lax.dynamic_slice_in_dim(all_out, row_start, req_dev, 0)
    own_query = queries.reshape(req_dev, step_count, kv_dev, group_size, HD)
    new_scores = (
        jnp.einsum("rskgd,rtkd->rkgst", own_query, new_keys, preferred_element_type=jnp.float32)
        * score_scale
    )
    causal = (
        jnp.arange(step_count, dtype=jnp.int32)[None, :]
        <= jnp.arange(step_count, dtype=jnp.int32)[:, None]
    )
    new_masked = jnp.where(causal, new_scores, negative_fill)
    highest = jnp.maximum(remote_highest, new_masked.max(axis=4))
    carried = jnp.exp(remote_highest - highest)
    new_weights = jnp.where(causal, jnp.exp(new_masked - highest[..., None]), 0.0)
    weight_total = remote_total * carried + new_weights.sum(axis=4)
    numerator = remote_out * carried[..., None] + jnp.einsum(
        "rkgst,rtkd->rkgsd",
        new_weights.astype(jnp.bfloat16),
        new_values,
        preferred_element_type=jnp.float32,
    )
    result = numerator / weight_total[..., None]
    return (
        jnp.transpose(result, (0, 3, 1, 2, 4))
        .reshape(req_dev, step_count, query_cols)
        .astype(jnp.bfloat16)
    )


def solution(mesh):
    placed = (
        P("inst", None, "tensor"),
        P("inst", None, "tensor"),
        P(None, "tensor"),
        P(None, "tensor"),
        P("inst", None, "tensor"),
        P("inst", None, "tensor"),
        P(),
        P(),
    )
    return jax.shard_map(
        on_device, mesh=mesh, in_specs=placed, out_specs=P("inst", None, "tensor"), check_vma=False
    )
```

profile of v0, /device:TPU:4, one launch (start us, length us, event | category | flops | bytes accessed | tf_op | source)
XLA Modules:
  0.0 348.4 jit_solution(10189655948921955028)
XLA Ops:
  6.5 3.2 fusion.21
  10.7 52.5 %all_gather.24 = bf16[32,4,1024]{2,1,0:T(4,128)(2,1)S(1)} all-gather(bf16[1,4,1024]{2,1,0:T(4,128)(2,1)} %param.10), channel_id=1, replica_groups=mesh['inst'=32,'tensor'=8] {'inst'}, dimensions={0}, use_global_device_ids=true | all-gather | bytes 270336 | tf_op jit(solution)/shard_map/all_gather | solution.py:46
  64.5 5.1 %fusion.11 = (f32[64,8,4]{1,2,0:T(4,128)S(1)}, f32[64,4,8,256]{3,2,1,0:T(8,128)}) fusion(pred[64,256]{1,0:T(8,128)(4,1)S(1)} %add_compare_fusion, bf16[64,256,128]{2,1,0:T(8,128)(2,1)} %param.14, bf16[64,4,8,128]{3,2,1,0:T(8,128)(2,1)S(1)} %gather.13, pred[64]{0:T(512)(128)(4,1)S(1)} %compare_and_fusion), kind=kOutput, calls=%fused_computation.21 | convolution fusion | flops 136050688 | bytes 6840384 | tf_op jit(solution)/shard_map/bskgd,bpkd->bkgsp/dot_general | solution.py:64
  70.7 3.7 %fusion.6 = f32[64,8,4,128]{3,1,2,0:T(8,128)S(1)} fusion(bf16[64,256,128]{2,1,0:T(8,128)(2,1)} %param.15, f32[64,4,8,256]{3,2,1,0:T(8,128)} %get-tuple-element.109, f32[64,8,4]{1,2,0:T(4,128)S(1)} %broadcast_select_fusion, pred[64,256]{1,0:T(8,128)(4,1)S(1)} %add_compare_fusion), kind=kOutput, calls=%fused_computation.14 | convolution fusion | flops 136839168 | bytes 7364608 | tf_op jit(solution)/shard_map/bkgsp,bpkd->bkgsd/dot_general | solution.py:77
  74.4 2.0 fusion.24
  76.5 2.5 fusion.13
  79.4 52.1 %all-gather.1 = f32[1024,8,4]{1,2,0:T(4,128)S(1)} all-gather(f32[32,8,4]{1,2,0:T(4,128)S(1)} %copy.85), channel_id=3, replica_groups=mesh['inst'=32,'tensor'=8] {'inst'}, dimensions={0}, use_global_device_ids=true | all-gather | bytes 135168 | tf_op jit(solution)/shard_map/all_gather | solution.py:15
  131.5 1.4 slice.38
  133.0 2.6 copy.93
  135.6 52.8 %all-gather = f32[1024,8,4]{1,2,0:T(4,128)S(1)} all-gather(f32[32,8,4]{1,2,0:T(4,128)S(1)} %select_reduce_fusion), channel_id=2, replica_groups=mesh['inst'=32,'tensor'=8] {'inst'}, dimensions={0}, use_global_device_ids=true | all-gather | bytes 135168 | tf_op jit(solution)/shard_map/all_gather | solution.py:15
  188.5 1.4 slice.37
  190.0 2.3 copy.92
  192.4 11.7 %all-gather.3 = bf16[1,4,8192]{2,1,0:T(4,128)(2,1)S(1)} all-gather(bf16[1,4,1024]{2,1,0:T(4,128)(2,1)S(1)} %copy-done.2), channel_id=5, replica_groups=mesh['inst'=32,'tensor'=8] {'tensor'}, dimensions={2}, use_global_device_ids=true | all-gather | bytes 73728 | tf_op jit(solution)/shard_map/all_gather | solution.py:41
  204.1 2.1 convolution_multiply_fusion
  206.3 20.2 %all-gather.6.cloned.1.call-done = f32[1024,8,4,128]{3,0,2,1:T(8,128)} async-done(((f32[32,8,4,128]{3,0,2,1:T(8,128)}), f32[1024,8,4,128]{3,0,2,1:T(8,128)}) %all-gather.6.cloned.1.call-update) | async-done | bytes 16777232 | tf_op jit(solution)/shard_map/all_gather | solution.py:15
  228.0 11.2 %slice.39 = f32[992,8,4,128]{3,0,2,1:T(8,128)} slice(f32[1024,8,4,128]{3,0,2,1:T(8,128)} %all-gather.6.cloned.1.call-done), slice={[32:1024], [0:8], [0:4], [0:128]} | slice | bytes 32505856 | tf_op jit(solution)/shard_map/slice | solution.py:17
  239.2 100.8 %while.14 = (s32[]{:T(128)}, f32[32,1,8,4]{0,3,2,1:T(4,128)S(1)}, f32[32,1,8,4]{0,3,2,1:T(4,128)S(1)}, f32[32,1,8,4,128]{4,3,2,1,0:T(4,128)S(1)}, f32[31,32,1,8,...) while((s32[]{:T(128)}, f32[32,1,8,4]{0,3,2,1:T(4,128)S(1)}, ...), condition=%wide.region_8.9_spmd, body=%wide.region_7.8_spmd.sunk | while | flops 400386 | bytes 2699369 | solution.py:18
  240.3 1.1 constant_dynamic-slice_fusion.2
  243.5 1.1 constant_dynamic-slice_fusion.2
  246.8 1.1 constant_dynamic-slice_fusion.2
  250.0 1.1 constant_dynamic-slice_fusion.2
  253.3 1.1 constant_dynamic-slice_fusion.2
  256.5 1.1 constant_dynamic-slice_fusion.2
  259.8 1.1 constant_dynamic-slice_fusion.2
  263.0 1.1 constant_dynamic-slice_fusion.2
  266.3 1.1 constant_dynamic-slice_fusion.2
  269.5 1.1 constant_dynamic-slice_fusion.2
  272.8 1.1 constant_dynamic-slice_fusion.2
  276.0 1.1 constant_dynamic-slice_fusion.2
  279.3 1.1 constant_dynamic-slice_fusion.2
  282.6 1.1 constant_dynamic-slice_fusion.2
  285.8 1.1 constant_dynamic-slice_fusion.2
  289.1 1.1 constant_dynamic-slice_fusion.2
  292.3 1.1 constant_dynamic-slice_fusion.2
  295.6 1.1 constant_dynamic-slice_fusion.2
  298.8 1.1 constant_dynamic-slice_fusion.2
  302.1 1.1 constant_dynamic-slice_fusion.2
  305.3 1.1 constant_dynamic-slice_fusion.2
  308.6 1.1 constant_dynamic-slice_fusion.2
  311.8 1.1 constant_dynamic-slice_fusion.2
  315.1 1.1 constant_dynamic-slice_fusion.2
  318.3 1.1 constant_dynamic-slice_fusion.2
  321.6 1.1 constant_dynamic-slice_fusion.2
  324.8 1.1 constant_dynamic-slice_fusion.2
  328.1 1.1 constant_dynamic-slice_fusion.2
  331.4 1.1 constant_dynamic-slice_fusion.2
  334.6 1.1 constant_dynamic-slice_fusion.2
  337.9 1.1 constant_dynamic-slice_fusion.2
  (227 shorter events, 72.6 us)
Async XLA Ops:
  6.5 333.9 %copy-start = (bf16[8192,128]{1,0:T(8,128)(2,1)S(1)}, bf16[8192,128]{1,0:T(8,128)(2,1)}, u32[]{:S(2)}) copy-start(bf16[8192,128]{1,0:T(8,128)(2,1)} %param.13) | copy-start | bytes 6291460
  6.5 220.0 %all-gather.6.cloned.1.call-start = ((), (), s32[]{:S(2)}) async-start(), calls=%async_computation | async-start | bytes 17301504 | tf_op jit(solution)/shard_map/all_gather | solution.py:15
  189.9 2.4 copy-start.2
  189.9 14.2 %copy-start.1 = (bf16[1,4,1024]{2,1,0:T(4,128)(2,1)S(1)}, bf16[1,4,1024]{2,1,0:T(4,128)(2,1)}, u32[]{:S(2)}) copy-start(bf16[1,4,1024]{2,1,0:T(4,128)(2,1)} %param.10) | copy-start | bytes 24580
Sparse Core Ops, SparseCore 0:
  76.6 149.8 all-gather.5
where the time goes:
time: 353 us; the launch traced here: 348 us
  blocking collectives  169 us (48%)
  local copies, waits for them, and re-layouts  66.3 us (19%)
  other arithmetic  64.1 us (18%)
  waiting for transfers between devices  20.3 us (6%)
  matrix products  13.8 us (4%)
  between operations  13.6 us (4%)
    all_gather x2, blocking collectives, combined_all(): pieces = jax.tree.map(lambda part: lax.all_gather(part, axis), value)  105 us
    all_gather x1, blocking collectives, on_device(): every_query = lax.all_gather(queries, 'inst', axis=0, tiled=True)  52.5 us
    dynamic_slice x31, local copies, waits for them, and re-layouts, combined_all(): lax.scan(lambda subtotal, slab: (join(subtotal, slab), None), head, tail)  33.8 us
    add x31, other arithmetic, join_parts(): this_part[2] * this_scale[..., None]  32.8 us
    mul x31, other arithmetic, join_parts(): other_part[2] * other_scale[..., None]  23.4 us
    all_gather x1, waiting for transfers between devices, combined_all(): pieces = jax.tree.map(lambda part: lax.all_gather(part, axis), value)  20.2 us
    slice x3, local copies, waits for them, and re-layouts, combined_all(): tail = jax.tree.map(lambda part: part[1:], pieces)  14.1 us
    all_gather x1, blocking collectives, on_device(): shard_piece = lax.all_gather(state_rows, 'tensor', axis=1, tiled=True)  11.7 us
  transfers between devices with their start and end apart: 1, of which 1 were waited for; matrix products, arithmetic and copies ran while one was open for 4% of the time, Pallas kernels for 0%

commit v1 on v0

v1 whole, which is shorter than its diff:
```python
import math

import jax
import jax.numpy as jnp
from jax import lax
from jax.experimental import pallas as pl
from jax.experimental.pallas import tpu as pltpu
from jax.sharding import PartitionSpec as P

HD = 128
STEPS = 4
GROUP = 8
ROWS = STEPS * GROUP
PAGE = 256
SLOTS = 64
CHUNK = 8
CHUNKS = SLOTS // CHUNK
LENT = 16
NY = 4
NZ = 8
NT = 8
NEG = -1e30
LOG2E_SCALE = math.log2(math.e) / math.sqrt(HD)
F32 = jnp.float32
BF16 = jnp.bfloat16
MESH = pl.DeviceIdType.MESH
NT_DIMS = (((1,), (1,)), ((), ()))


def kernel(
    len_smem, tab_smem, tab_ref, q_hbm, st_hbm, kw_hbm, vw_hbm, k_hbm, v_hbm,
    out_ref,
    q_raw, st_raw, rows_f32, k_buf, v_buf, kw_buf, vw_buf, s_buf, bias_buf,
    st_all, q_z, q2_send, q2_recv, p_z, p2_send, p2_recv,
    small_sem, k_sem, v_sem, w_sem,
    st_send_sem, st_recv_sem, qz_send_sem, qz_recv_sem, q2_send_sem, q2_recv_sem,
    pz_send_sem, pz_recv_sem, p2_send_sem, p2_recv_sem,
):
    inst = lax.axis_index("inst")
    tensor = lax.axis_index("tensor")
    z = inst // NY
    y = inst % NY
    z_peer = [((z + d) % NZ) * NY + y for d in range(NZ)]
    y_peer = [z * NY + (y + e) % NY for e in range(NY)]
    t_peer = [(tensor + d) % NT for d in range(NT)]

    barrier = pltpu.get_barrier_semaphore()
    for d in range(1, NZ):
        pl.semaphore_signal(barrier, inc=1, device_id=(z_peer[d], tensor), device_id_type=MESH)
    for e in range(1, NY):
        pl.semaphore_signal(barrier, inc=1, device_id=(y_peer[e], tensor), device_id_type=MESH)
    for d in range(1, NT):
        pl.semaphore_signal(barrier, inc=1, device_id=(inst, t_peer[d]), device_id_type=MESH)

    q_copy = pltpu.make_async_copy(q_hbm, q_raw, small_sem.at[0])
    st_copy = pltpu.make_async_copy(st_hbm, st_raw, small_sem.at[1])
    q_copy.start()
    st_copy.start()

    def k_copy(c):
        part = pl.ds(c * CHUNK, CHUNK)
        return pltpu.make_async_copy(k_hbm.at[part], k_buf.at[part], k_sem.at[c])

    def v_copy(c):
        part = pl.ds(c * CHUNK, CHUNK)
        return pltpu.make_async_copy(v_hbm.at[part], v_buf.at[part], v_sem.at[c])

    for c in range(CHUNKS):
        k_copy(c).start()
    for c in range(CHUNKS):
        v_copy(c).start()
    w_copies = [
        pltpu.make_async_copy(kw_hbm, kw_buf, w_sem.at[0]),
        pltpu.make_async_copy(vw_hbm, vw_buf, w_sem.at[1]),
    ]
    for copy in w_copies:
        copy.start()

    def to_rows(raw):
        wide = raw[0].astype(F32)
        for g in range(GROUP):
            rows_f32[g * STEPS:(g + 1) * STEPS, :] = wide[:, g * HD:(g + 1) * HD]
        return rows_f32[...].astype(BF16)

    q_copy.wait()
    q_z[0] = to_rows(q_raw)
    st_copy.wait()
    st_all[0] = to_rows(st_raw)

    pl.semaphore_wait(barrier, NZ + NY + NT - 3)

    qz_copies = [
        pltpu.make_async_remote_copy(
            src_ref=q_z.at[0], dst_ref=q_z.at[d], send_sem=qz_send_sem.at[d], recv_sem=qz_recv_sem.at[d],
            device_id=(z_peer[d], tensor), device_id_type=MESH)
        for d in range(1, NZ)
    ]
    st_copies = [
        pltpu.make_async_remote_copy(
            src_ref=st_all.at[0], dst_ref=st_all.at[d], send_sem=st_send_sem.at[d], recv_sem=st_recv_sem.at[d],
            device_id=(inst, t_peer[d]), device_id_type=MESH)
        for d in range(1, NT)
    ]
    for copy in qz_copies + st_copies:
        copy.start()

    table = tab_ref[...]
    holder = table >> 6
    row_id = lax.broadcasted_iota(jnp.int32, table.shape, 0)
    page_id = lax.broadcasted_iota(jnp.int32, table.shape, 1)
    lent_code = jnp.where((table >= 0) & (holder != row_id), row_id * SLOTS + (SLOTS - 1) - page_id, -1)
    lent_holder = jnp.where((table >= 0) & (holder != row_id), holder, -1)
    guest_code = [jnp.max(jnp.where(holder == y_peer[e], lent_code, -1)) for e in range(NY)]
    lender = [jnp.max(jnp.where(row_id == y_peer[e], lent_holder, -1)) for e in range(NY)]

    own_length = len_smem[0, inst]
    own_row = jnp.broadcast_to(tab_ref[pl.ds(inst, 1), :] - inst * SLOTS, (SLOTS, SLOTS))
    slot_id = lax.broadcasted_iota(jnp.int32, (SLOTS, SLOTS), 0)
    page_of = lax.broadcasted_iota(jnp.int32, (SLOTS, SLOTS), 1)
    counted = jnp.clip(own_length - page_of * PAGE, 0, PAGE).astype(F32)
    valid = jnp.sum(jnp.where(own_row == slot_id, counted, 0.0), axis=1, keepdims=True)
    token = lax.broadcasted_iota(jnp.int32, (SLOTS, PAGE), 1).astype(F32)
    bias_buf[...] = jnp.where(token < valid, 0.0, NEG)

    query = q_z[0]

    def scores_chunk(c, top):
        k_copy(c).wait()
        for p in range(CHUNK):
            slot = c * CHUNK + p
            s = lax.dot_general(query, k_buf[slot], NT_DIMS, preferred_element_type=F32)
            s = s + bias_buf[pl.ds(slot, 1), :]
            s_buf[c, :, p * PAGE:(p + 1) * PAGE] = s
            top = jnp.maximum(top, jnp.maximum(s[:, :HD], s[:, HD:]))
        return top

    top = lax.fori_loop(0, CHUNKS, scores_chunk, jnp.full((ROWS, HD), NEG, F32))
    own_top = jnp.max(top, axis=1, keepdims=True) * LOG2E_SCALE

    for copy in qz_copies:
        copy.wait_recv()
    for e in range(NY):
        picked = q_z[(z - (guest_code[e] >> 8)) & (NZ - 1)]
        if e == 0:
            q2_recv[0] = picked
        else:
            q2_send[e] = picked
    q2_copies = [
        pltpu.make_async_remote_copy(
            src_ref=q2_send.at[e], dst_ref=q2_recv.at[e], send_sem=q2_send_sem.at[e], recv_sem=q2_recv_sem.at[e],
            device_id=(y_peer[e], tensor), device_id_type=MESH)
        for e in range(1, NY)
    ]
    for copy in q2_copies:
        copy.start()

    def lanes_sum(w):
        total = w[:, :HD]
        for b in range(1, w.shape[1] // HD):
            total = total + w[:, b * HD:(b + 1) * HD]
        return total

    def values_chunk(c, carry):
        total, numerator = carry
        v_copy(c).wait()
        half = CHUNK // 2
        for h in range(2):
            s = s_buf[c, :, h * half * PAGE:(h + 1) * half * PAGE]
            w = jnp.exp2(s * LOG2E_SCALE - own_top)
            total = total + lanes_sum(w)
            v = v_buf[pl.ds(c * CHUNK + h * half, half)].reshape(half * PAGE, HD)
            numerator = numerator + jnp.dot(w.astype(BF16), v, preferred_element_type=F32)
        return total, numerator

    total, own_out = lax.fori_loop(
        0, CHUNKS, values_chunk, (jnp.zeros((ROWS, HD), F32), jnp.zeros((ROWS, HD), F32)))
    own_total = jnp.sum(total, axis=1, keepdims=True)

    guest = guest_code[0] >> 6
    first_page = (SLOTS - 1) - (guest_code[0] & (SLOTS - 1))
    guest_row = jnp.maximum(guest, 0)
    guest_length = jnp.where(guest >= 0, len_smem[0, guest_row], 0)
    guest_pages = ((guest_length + PAGE - 1) // PAGE) // 4
    page_token = lax.broadcasted_iota(jnp.int32, (1, PAGE), 1)
    slots = []
    limits = []
    for i in range(LENT):
        page = jnp.minimum(first_page + i, SLOTS - 1)
        slots.append(jnp.clip(tab_smem[guest_row, page] - inst * SLOTS, 0, SLOTS - 1))
        limits.append(jnp.where(i < guest_pages, guest_length - page * PAGE, 0))

    for copy in q2_copies:
        copy.wait_recv()
    guest_query = q2_recv[(y - guest) & (NY - 1)]
    guest_top = jnp.full((ROWS, HD), NEG, F32)
    for i in range(LENT):
        s = lax.dot_general(guest_query, k_buf[slots[i]], NT_DIMS, preferred_element_type=F32)
        s = jnp.where(page_token < limits[i], s, NEG)
        s_buf[i // CHUNK, :, (i % CHUNK) * PAGE:(i % CHUNK + 1) * PAGE] = s
        guest_top = jnp.maximum(guest_top, jnp.maximum(s[:, :HD], s[:, HD:]))
    guest_top = jnp.max(guest_top, axis=1, keepdims=True) * LOG2E_SCALE
    total = jnp.zeros((ROWS, HD), F32)
    guest_out = jnp.zeros((ROWS, HD), F32)
    for i in range(LENT):
        s = s_buf[i // CHUNK, :, (i % CHUNK) * PAGE:(i % CHUNK + 1) * PAGE]
        w = jnp.exp2(s * LOG2E_SCALE - guest_top)
        total = total + lanes_sum(w)
        guest_out = guest_out + jnp.dot(w.astype(BF16), v_buf[slots[i]], preferred_element_type=F32)
    guest_total = jnp.sum(total, axis=1, keepdims=True)
    level = jnp.broadcast_to(guest_top + jnp.log2(guest_total), (ROWS, HD))
    lane = lax.broadcasted_iota(jnp.int32, (ROWS, HD), 1)
    high = level.astype(BF16).astype(F32)
    middle = (level - high).astype(BF16).astype(F32)
    low = level - high - middle
    place = lane & 63
    coded = jnp.where(place == 0, high, jnp.where(place == 1, middle, jnp.where(place == 2, low, 0.0)))
    half_rows = ROWS // 2
    coded = jnp.where(lane[:half_rows] < 64, coded[:half_rows], coded[half_rows:])
    p_z[0, :ROWS, :] = (guest_out / guest_total).astype(BF16)
    p_z[0, ROWS:, :] = coded.astype(BF16)
    pz_copies = [
        pltpu.make_async_remote_copy(
            src_ref=p_z.at[0], dst_ref=p_z.at[d], send_sem=pz_send_sem.at[d], recv_sem=pz_recv_sem.at[d],
            device_id=(z_peer[d], tensor), device_id_type=MESH)
        for d in range(1, NZ)
    ]
    for copy in pz_copies:
        copy.start()

    for copy in w_copies:
        copy.wait()
    for copy in st_copies:
        copy.wait_recv()
    row16 = lax.broadcasted_iota(jnp.int32, (16, HD), 0) // STEPS

    def project(d, acc):
        source = (tensor - d + NT) % NT
        for h in range(2):
            x = st_all[d, h * 16:(h + 1) * 16, :].astype(F32)
            left = jnp.concatenate([jnp.where(row16 == g, x, 0.0) for g in range(4)], axis=1).astype(BF16)
            weight = jnp.concatenate(
                [kw_buf[source, h * 512:(h + 1) * 512, :], vw_buf[source, h * 512:(h + 1) * 512, :]], axis=1)
            acc = acc + jnp.dot(left, weight, preferred_element_type=F32)
        return acc

    acc = lax.fori_loop(0, NT, project, jnp.zeros((16, 2 * HD), F32))
    acc = acc[:8] + acc[8:]
    acc = acc[:4] + acc[4:]
    padded = jnp.concatenate([acc, jnp.zeros((12, 2 * HD), F32)], axis=0).astype(BF16)
    new_keys = padded[:, :HD]
    new_values = padded[:, HD:]
    s = lax.dot_general(query, new_keys, NT_DIMS, preferred_element_type=F32)
    step = lax.broadcasted_iota(jnp.int32, (ROWS, 16), 0) % STEPS
    other = lax.broadcasted_iota(jnp.int32, (ROWS, 16), 1)
    s = jnp.where(other <= step, s * LOG2E_SCALE, NEG)
    merged_top = jnp.maximum(own_top, jnp.max(s, axis=1, keepdims=True))
    w = jnp.exp2(s - merged_top)
    kept = jnp.exp2(own_top - merged_top)
    merged_total = own_total * kept + jnp.sum(w, axis=1, keepdims=True)
    merged_out = own_out * kept + jnp.dot(w.astype(BF16), new_values, preferred_element_type=F32)

    for copy in pz_copies:
        copy.wait_recv()
    for e in range(NY):
        picked = p_z[(z - (lender[e] >> 2)) & (NZ - 1)]
        if e == 0:
            p2_recv[0] = picked
        else:
            p2_send[e] = picked
    p2_copies = [
        pltpu.make_async_remote_copy(
            src_ref=p2_send.at[e], dst_ref=p2_recv.at[e], send_sem=p2_send_sem.at[e], recv_sem=p2_recv_sem.at[e],
            device_id=(y_peer[e], tensor), device_id_type=MESH)
        for e in range(1, NY)
    ]
    for copy in p2_copies:
        copy.start()
    for copy in p2_copies:
        copy.wait_recv()
    lent = p2_recv[(y - lender[0]) & (NY - 1)].astype(F32)
    coded = lent[ROWS:]
    lane16 = lane[:half_rows]
    level = jnp.concatenate([
        jnp.sum(jnp.where(lane16 < 64, coded, 0.0), axis=1, keepdims=True),
        jnp.sum(jnp.where(lane16 < 64, 0.0, coded), axis=1, keepdims=True)], axis=0)
    level = jnp.where(lender[0] >= 0, level, NEG)
    highest = jnp.maximum(merged_top, level)
    kept = jnp.exp2(merged_top - highest)
    added = jnp.exp2(level - highest)
    out_ref[...] = (merged_out * kept + lent[:ROWS] * added) / (merged_total * kept + added)

    for copy in qz_copies + st_copies + q2_copies + pz_copies + p2_copies:
        copy.wait_send()


def on_device(queries, new_states, key_weight, value_weight, key_pool, value_pool, lengths, page_table):
    hbm = pl.BlockSpec(memory_space=pltpu.HBM)
    dma = pltpu.SemaphoreType.DMA
    out = pl.pallas_call(
        kernel,
        out_shape=jax.ShapeDtypeStruct((ROWS, HD), F32),
        in_specs=[
            pl.BlockSpec(memory_space=pltpu.SMEM),
            pl.BlockSpec(memory_space=pltpu.SMEM),
            pl.BlockSpec(memory_space=pltpu.VMEM),
            hbm, hbm, hbm, hbm, hbm, hbm,
        ],
        out_specs=pl.BlockSpec(memory_space=pltpu.VMEM),
        scratch_shapes=[
            pltpu.VMEM((1, STEPS, GROUP * HD), BF16),
            pltpu.VMEM((1, STEPS, GROUP * HD), BF16),
            pltpu.VMEM((ROWS, HD), F32),
            pltpu.VMEM((SLOTS, PAGE, HD), BF16),
            pltpu.VMEM((SLOTS, PAGE, HD), BF16),
            pltpu.VMEM((NT, GROUP * HD, HD), BF16),
            pltpu.VMEM((NT, GROUP * HD, HD), BF16),
            pltpu.VMEM((CHUNKS, ROWS, CHUNK * PAGE), F32),
            pltpu.VMEM((SLOTS, PAGE), F32),
            pltpu.VMEM((NT, ROWS, HD), BF16),
            pltpu.VMEM((NZ, ROWS, HD), BF16),
            pltpu.VMEM((NY, ROWS, HD), BF16),
            pltpu.VMEM((NY, ROWS, HD), BF16),
            pltpu.VMEM((NZ, ROWS + 16, HD), BF16),
            pltpu.VMEM((NY, ROWS + 16, HD), BF16),
            pltpu.VMEM((NY, ROWS + 16, HD), BF16),
            dma((2,)), dma((CHUNKS,)), dma((CHUNKS,)), dma((2,)),
            dma((NT,)), dma((NT,)), dma((NZ,)), dma((NZ,)), dma((NY,)), dma((NY,)),
            dma((NZ,)), dma((NZ,)), dma((NY,)), dma((NY,)),
        ],
        compiler_params=pltpu.CompilerParams(
            collective_id=0, has_side_effects=True, vmem_limit_bytes=48 * 1024 * 1024),
    )(
        lengths.reshape(1, -1), page_table, page_table, queries, new_states,
        key_weight.reshape(NT, GROUP * HD, HD), value_weight.reshape(NT, GROUP * HD, HD),
        key_pool, value_pool,
    )
    return (
        jnp.transpose(out.reshape(GROUP, STEPS, HD), (1, 0, 2))
        .reshape(1, STEPS, GROUP * HD)
        .astype(BF16)
    )


def solution(mesh):
    placed = (
        P("inst", None, "tensor"),
        P("inst", None, "tensor"),
        P(None, "tensor"),
        P(None, "tensor"),
        P("inst", None, "tensor"),
        P("inst", None, "tensor"),
        P(),
        P(),
    )
    return jax.shard_map(
        on_device, mesh=mesh, in_specs=placed, out_specs=P("inst", None, "tensor"), check_vma=False
    )
```

time: 353 us -> 35.3 us (0.10); the launches traced: 348 us -> 35 us
  blocking collectives: 169 us -> 0 us
  other arithmetic: 64.1 us -> 0.6 us
  local copies, waits for them, and re-layouts: 66.3 us -> 5.95 us
  Pallas kernels: 0 us -> 28.4 us
  waiting for transfers between devices: 20.3 us -> 0 us
  matrix products: 13.8 us -> 0 us
  between operations: 13.6 us -> 0.02 us
    all_gather x4 -> x0, blocking collectives: 169 us -> none  [the longest x2 105 us: combined_all(): pieces = jax.tree.map(lambda part: lax.all_gather(part, axis), value)]
    dynamic_slice x31 -> x0, local copies, waits for them, and re-layouts: 33.8 us -> none  [combined_all(): lax.scan(lambda subtotal, slab: (join(subtotal, slab), None), head, tail)]
    add x32 -> x0, other arithmetic: 32.8 us -> none  [the longest x31 32.8 us: join_parts(): this_part[2] * this_scale[..., None]]
    pallas_call x0 -> x1, Pallas kernels: none -> 28.4 us  [on_device(): pl.pallas_call(kernel, out_shape=jax.ShapeDtypeStruct((ROWS, HD), F32), i...]
    mul x64 -> x0, other arithmetic: 24 us -> none  [the longest x31 23.4 us: join_parts(): other_part[2] * other_scale[..., None]]
    all_gather x1 -> x0, waiting for transfers between devices: 20.2 us -> none  [combined_all(): pieces = jax.tree.map(lambda part: lax.all_gather(part, axis), value)]
    slice x3 -> x0, local copies, waits for them, and re-layouts: 14.1 us -> none  [combined_all(): tail = jax.tree.map(lambda part: part[1:], pieces)]
    dot_general x6 -> x0, matrix products: 13.8 us -> none  [the longest x1 5.08 us: on_device(): jnp.einsum('bskgd,bpkd->bkgsp', page_queries, page_keys, preferred_elemen...]
  transfers between devices with their start and end apart: 1 -> 0, of which waited for: 1 -> 0; matrix products, arithmetic and copies ran while one was open for 4% -> 0% of each run, Pallas kernels for 0% -> 0%
where the time goes in v1:
time: 35.3 us; the launch traced here: 35 us
  Pallas kernels  28.4 us (80%)
  local copies, waits for them, and re-layouts  5.95 us (17%)
  other arithmetic  0.6 us (2%)
    pallas_call x1, Pallas kernels, on_device(): pl.pallas_call(kernel, out_shape=jax.ShapeDtypeStruct((ROWS, HD), F32), i...  28.4 us
    unnamed x12, local copies, waits for them, and re-layouts  5.95 us

profile of v1, /device:TPU:4, one launch (start us, length us, event | category | flops | bytes accessed | tf_op | source)
XLA Modules:
  0.0 35.0 jit_solution(307803706693535970)
XLA Ops:
  0.0 0.0 copy-start
  0.0 1.6 %copy-done = bf16[8192,128]{1,0:T(8,128)(2,1)S(1)} copy-done((bf16[8192,128]{1,0:T(8,128)(2,1)S(1)}, bf16[8192,128]{1,0:T(8,128)(2,1)}, u32[]{:S(2)}) %copy-start) | copy-done | bytes 2097176
  1.6 0.0 copy-start.1
  1.6 1.6 %copy-done.1 = bf16[8192,128]{1,0:T(8,128)(2,1)S(1)} copy-done((bf16[8192,128]{1,0:T(8,128)(2,1)S(1)}, bf16[8192,128]{1,0:T(8,128)(2,1)}, u32[]{:S(2)}) %copy-start.1) | copy-done | bytes 2097176
  3.2 0.0 copy-start.2
  3.2 0.7 %copy-done.2 = s32[32,64]{1,0:T(8,128)S(1)} copy-done((s32[32,64]{1,0:T(8,128)S(1)}, s32[32,64]{1,0:T(8,128)}, u32[]{:S(2)}) %copy-start.2) | copy-done | bytes 8216
  3.9 0.0 copy-start.3
  3.9 0.7 %copy-done.3 = bf16[1,4,1024]{2,1,0:T(4,128)(2,1)S(1)} copy-done((bf16[1,4,1024]{2,1,0:T(4,128)(2,1)S(1)}, bf16[1,4,1024]{2,1,0:T(4,128)(2,1)}, u32[]{:S(2)}) %copy-start.3) | copy-done | bytes 8216
  4.6 0.0 copy-start.4
  4.6 0.7 %copy-done.4 = bf16[1,4,1024]{2,1,0:T(4,128)(2,1)S(1)} copy-done((bf16[1,4,1024]{2,1,0:T(4,128)(2,1)S(1)}, bf16[1,4,1024]{2,1,0:T(4,128)(2,1)}, u32[]{:S(2)}) %copy-start.4) | copy-done | bytes 8216
  5.3 0.0 copy-start.5
  5.3 0.7 %copy-done.5 = s32[32]{0:T(128)S(1)} copy-done((s32[32]{0:T(128)S(1)}, s32[32]{0:T(128)}, u32[]{:S(2)}) %copy-start.5) | copy-done | bytes 152
  6.0 28.4 %shard_map.82 = f32[32,128]{1,0:T(8,128)S(1)} custom-call(s32[1,32]{1,0:T(1,128)S(1)} %bitcast.10, s32[32,64]{1,0:T(8,128)S(1)} %copy-done.2, s32[32,64]{1,0:T(8,128)S(1)} %copy-done.2, bf16[1,4,1024]{2,1,0:T(4,128)(2,1)S(1)} %copy-done.3, bf16[1,4,1024]{2,1,0:T(4,128)(2,1)S(1)} %copy-done.4, bf16[8,1024,128]{2,1,0:T(8,128)(2,1)S(1)} %bitcast.8, ...), custom_call_target="tpu_custom_call" | custom-call | tf_op jit(solution)/shard_map/pallas_call | solution.py:299
  34.4 0.6 %convert_element_type.20 = bf16[32,128]{1,0:T(8,128)(2,1)} convert(f32[32,128]{1,0:T(8,128)S(1)} %shard_map.82) | non-fusion elementwise | flops 4096 | bytes 24576 | tf_op jit(solution)/shard_map/convert_element_type | solution.py:340
Async XLA Ops:
  0.0 1.6 %copy-start = (bf16[8192,128]{1,0:T(8,128)(2,1)S(1)}, bf16[8192,128]{1,0:T(8,128)(2,1)}, u32[]{:S(2)}) copy-start(bf16[8192,128]{1,0:T(8,128)(2,1)} %param.10) | copy-start | bytes 6291460
  1.6 1.6 %copy-start.1 = (bf16[8192,128]{1,0:T(8,128)(2,1)S(1)}, bf16[8192,128]{1,0:T(8,128)(2,1)}, u32[]{:S(2)}) copy-start(bf16[8192,128]{1,0:T(8,128)(2,1)} %param.11) | copy-start | bytes 6291460
  3.2 0.7 %copy-start.2 = (s32[32,64]{1,0:T(8,128)S(1)}, s32[32,64]{1,0:T(8,128)}, u32[]{:S(2)}) copy-start(s32[32,64]{1,0:T(8,128)} %tab_ref.1) | copy-start | bytes 24580
  3.9 0.7 %copy-start.3 = (bf16[1,4,1024]{2,1,0:T(4,128)(2,1)S(1)}, bf16[1,4,1024]{2,1,0:T(4,128)(2,1)}, u32[]{:S(2)}) copy-start(bf16[1,4,1024]{2,1,0:T(4,128)(2,1)} %q_hbm.1) | copy-start | bytes 24580
  4.6 0.7 %copy-start.4 = (bf16[1,4,1024]{2,1,0:T(4,128)(2,1)S(1)}, bf16[1,4,1024]{2,1,0:T(4,128)(2,1)}, u32[]{:S(2)}) copy-start(bf16[1,4,1024]{2,1,0:T(4,128)(2,1)} %st_hbm.1) | copy-start | bytes 24580
  5.3 0.7 %copy-start.5 = (s32[32]{0:T(128)S(1)}, s32[32]{0:T(128)}, u32[]{:S(2)}) copy-start(s32[32]{0:T(128)} %param.14) | copy-start | bytes 388

commit v2 on v1

v2 whole, which is shorter than its diff:
```python
import math

import jax
import jax.numpy as jnp
from jax import lax
from jax.experimental import pallas as pl
from jax.experimental.pallas import tpu as pltpu
from jax.sharding import PartitionSpec as P

HD = 128
STEPS = 4
GROUP = 8
ROWS = STEPS * GROUP
PAGE = 256
SLOTS = 64
CHUNK = 8
CHUNKS = SLOTS // CHUNK
LENT = 16
NY = 4
NZ = 8
NT = 8
NEG = -1e30
VMEM_BYTES = 60 * 1024 * 1024
Z_ORDER = (4, 3, 5, 2, 6, 1, 7)
Y_ORDER = (2, 1, 3)
T_ORDER = (4, 5, 3, 2, 6, 7, 1)
LOG2E_SCALE = math.log2(math.e) / math.sqrt(HD)
F32 = jnp.float32
BF16 = jnp.bfloat16
MESH = pl.DeviceIdType.MESH
NT_DIMS = (((1,), (1,)), ((), ()))


def kernel(
    len_hbm, tab_hbm, q_hbm, st_hbm, kw_hbm, vw_hbm, k_hbm, v_hbm,
    out_ref,
    len_smem, tab_smem, tab_ref, k_buf, v_buf, kw_buf, vw_buf, s_buf, guest_buf, bias_buf,
    st_all, q_z, q2_send, q2_recv, p_z, p2_send, p2_recv,
    small_sem, k_sem, v_sem, w_sem,
    st_send_sem, st_recv_sem, qz_send_sem, qz_recv_sem, q2_send_sem, q2_recv_sem,
    pz_send_sem, pz_recv_sem, p2_send_sem, p2_recv_sem,
):
    inst = lax.axis_index("inst")
    tensor = lax.axis_index("tensor")
    z = inst // NY
    y = inst % NY
    z_peer = [((z + d) % NZ) * NY + y for d in range(NZ)]
    y_peer = [z * NY + (y + e) % NY for e in range(NY)]
    t_peer = [(tensor + d) % NT for d in range(NT)]

    barrier = pltpu.get_barrier_semaphore()
    for d in Z_ORDER:
        pl.semaphore_signal(barrier, inc=1, device_id=(z_peer[d], tensor), device_id_type=MESH)
    for e in Y_ORDER:
        pl.semaphore_signal(barrier, inc=1, device_id=(y_peer[e], tensor), device_id_type=MESH)
    for d in T_ORDER:
        pl.semaphore_signal(barrier, inc=1, device_id=(inst, t_peer[d]), device_id_type=MESH)

    small_copies = [
        pltpu.make_async_copy(tab_hbm, tab_ref, small_sem.at[0]),
        pltpu.make_async_copy(q_hbm, q_z.at[0], small_sem.at[1]),
        pltpu.make_async_copy(st_hbm, st_all.at[0], small_sem.at[2]),
        pltpu.make_async_copy(len_hbm, len_smem, small_sem.at[3]),
        pltpu.make_async_copy(tab_hbm, tab_smem, small_sem.at[4]),
    ]
    for copy in small_copies:
        copy.start()

    def k_copy(c):
        part = pl.ds(c * CHUNK, CHUNK)
        return pltpu.make_async_copy(k_hbm.at[part], k_buf.at[part], k_sem.at[c])

    def v_copy(c):
        part = pl.ds(c * CHUNK, CHUNK)
        return pltpu.make_async_copy(v_hbm.at[part], v_buf.at[part], v_sem.at[c])

    for c in range(CHUNKS):
        k_copy(c).start()
    for c in range(CHUNKS):
        v_copy(c).start()
    w_copies = [
        pltpu.make_async_copy(kw_hbm, kw_buf, w_sem.at[0]),
        pltpu.make_async_copy(vw_hbm, vw_buf, w_sem.at[1]),
    ]
    for copy in w_copies:
        copy.start()

    small_copies[1].wait()
    small_copies[2].wait()
    pl.semaphore_wait(barrier, NZ + NY + NT - 3)

    qz_copies = [
        pltpu.make_async_remote_copy(
            src_ref=q_z.at[0], dst_ref=q_z.at[d], send_sem=qz_send_sem.at[d], recv_sem=qz_recv_sem.at[d],
            device_id=(z_peer[d], tensor), device_id_type=MESH)
        for d in Z_ORDER
    ]
    st_copies = [
        pltpu.make_async_remote_copy(
            src_ref=st_all.at[0], dst_ref=st_all.at[d], send_sem=st_send_sem.at[d], recv_sem=st_recv_sem.at[d],
            device_id=(inst, t_peer[d]), device_id_type=MESH)
        for d in T_ORDER
    ]
    for copy in qz_copies + st_copies:
        copy.start()

    small_copies[0].wait()
    small_copies[3].wait()
    small_copies[4].wait()
    table = tab_ref[...]
    holder = table >> 6
    row_id = lax.broadcasted_iota(jnp.int32, table.shape, 0)
    page_id = lax.broadcasted_iota(jnp.int32, table.shape, 1)
    lent = (table >= 0) & (holder != row_id)
    lent_code = jnp.where(lent, row_id * SLOTS + (SLOTS - 1) - page_id, -1)
    lent_holder = jnp.where(lent, holder, -1)
    guest_code = [jnp.max(jnp.where(holder == y_peer[e], lent_code, -1)) for e in range(NY)]
    lender = [jnp.max(jnp.where(row_id == y_peer[e], lent_holder, -1)) for e in range(NY)]

    own_length = len_smem[0, inst]
    own_row = jnp.broadcast_to(tab_ref[pl.ds(inst, 1), :] - inst * SLOTS, (SLOTS, SLOTS))
    slot_id = lax.broadcasted_iota(jnp.int32, (SLOTS, SLOTS), 0)
    page_of = lax.broadcasted_iota(jnp.int32, (SLOTS, SLOTS), 1)
    counted = jnp.clip(own_length - page_of * PAGE, 0, PAGE).astype(F32)
    valid = jnp.sum(jnp.where(own_row == slot_id, counted, 0.0), axis=1, keepdims=True)
    token = lax.broadcasted_iota(jnp.int32, (SLOTS, PAGE), 1).astype(F32)
    bias_buf[...] = jnp.where(token < valid, 0.0, NEG)

    guest = guest_code[0] >> 6
    first_page = (SLOTS - 1) - (guest_code[0] & (SLOTS - 1))
    guest_row = jnp.maximum(guest, 0)
    guest_length = jnp.where(guest >= 0, len_smem[0, guest_row], 0)
    guest_pages = ((guest_length + PAGE - 1) // PAGE) // 4
    page_token = lax.broadcasted_iota(jnp.int32, (1, PAGE), 1)
    slots = []
    limits = []
    for i in range(LENT):
        page = jnp.minimum(first_page + i, SLOTS - 1)
        slots.append(jnp.clip(tab_smem[guest_row, page] - inst * SLOTS, 0, SLOTS - 1))
        limits.append(jnp.where(i < guest_pages, guest_length - page * PAGE, 0))

    query = q_z[0]

    def scores_chunk(c, top):
        k_copy(c).wait()
        for p in range(CHUNK):
            slot = c * CHUNK + p
            s = lax.dot_general(query, k_buf[slot], NT_DIMS, preferred_element_type=F32)
            s = s + bias_buf[pl.ds(slot, 1), :]
            s_buf[c, :, p * PAGE:(p + 1) * PAGE] = s
            top = jnp.maximum(top, jnp.maximum(s[:, :HD], s[:, HD:]))
        return top

    def lanes_sum(w):
        total = w[:, :HD]
        for b in range(1, w.shape[1] // HD):
            total = total + w[:, b * HD:(b + 1) * HD]
        return total

    def values_chunk(c, carry):
        total, numerator = carry
        v_copy(c).wait()
        half = CHUNK // 2
        for h in range(2):
            s = s_buf[c, :, h * half * PAGE:(h + 1) * half * PAGE]
            w = jnp.exp2(s * LOG2E_SCALE - own_top)
            total = total + lanes_sum(w)
            v = v_buf[pl.ds(c * CHUNK + h * half, half)].reshape(half * PAGE, HD)
            numerator = numerator + jnp.dot(w.astype(BF16), v, preferred_element_type=F32)
        return total, numerator

    top = jnp.full((ROWS, HD), NEG, F32)
    top = lax.fori_loop(0, CHUNKS, scores_chunk, top)

    for copy in qz_copies:
        copy.wait_recv()
    q2_copies = []
    for e in Y_ORDER + (0,):
        picked = q_z[(z - (guest_code[e] >> 8)) & (NZ - 1)]
        if e == 0:
            q2_recv[0] = picked
        else:
            q2_send[e] = picked
            copy = pltpu.make_async_remote_copy(
                src_ref=q2_send.at[e], dst_ref=q2_recv.at[e], send_sem=q2_send_sem.at[e], recv_sem=q2_recv_sem.at[e],
                device_id=(y_peer[e], tensor), device_id_type=MESH)
            copy.start()
            q2_copies.append(copy)

    own_top = jnp.max(top, axis=1, keepdims=True) * LOG2E_SCALE

    carry = (jnp.zeros((ROWS, HD), F32), jnp.zeros((ROWS, HD), F32))
    carry = lax.fori_loop(0, CHUNKS, values_chunk, carry)
    total, own_out = carry
    own_total = jnp.sum(total, axis=1, keepdims=True)

    for copy in q2_copies:
        copy.wait_recv()
    guest_query = q2_recv[(y - guest) & (NY - 1)]
    guest_top = jnp.full((ROWS, HD), NEG, F32)
    for i in range(LENT):
        s = lax.dot_general(guest_query, k_buf[slots[i]], NT_DIMS, preferred_element_type=F32)
        s = jnp.where(page_token < limits[i], s, NEG)
        guest_buf[:, i * PAGE:(i + 1) * PAGE] = s
        guest_top = jnp.maximum(guest_top, jnp.maximum(s[:, :HD], s[:, HD:]))
    guest_top = jnp.max(guest_top, axis=1, keepdims=True) * LOG2E_SCALE
    total = jnp.zeros((ROWS, HD), F32)
    guest_out = jnp.zeros((ROWS, HD), F32)
    for i in range(LENT):
        s = guest_buf[:, i * PAGE:(i + 1) * PAGE]
        w = jnp.exp2(s * LOG2E_SCALE - guest_top)
        total = total + lanes_sum(w)
        guest_out = guest_out + jnp.dot(w.astype(BF16), v_buf[slots[i]], preferred_element_type=F32)
    guest_total = jnp.sum(total, axis=1, keepdims=True)
    level = jnp.broadcast_to(guest_top + jnp.log2(guest_total), (ROWS, HD))
    lane = lax.broadcasted_iota(jnp.int32, (ROWS, HD), 1)
    high = level.astype(BF16).astype(F32)
    middle = (level - high).astype(BF16).astype(F32)
    low = level - high - middle
    place = lane & 63
    coded = jnp.where(place == 0, high, jnp.where(place == 1, middle, jnp.where(place == 2, low, 0.0)))
    half_rows = ROWS // 2
    coded = jnp.where(lane[:half_rows] < 64, coded[:half_rows], coded[half_rows:])
    p_z[0, :ROWS, :] = (guest_out / guest_total).astype(BF16)
    p_z[0, ROWS:, :] = coded.astype(BF16)
    pz_copies = [
        pltpu.make_async_remote_copy(
            src_ref=p_z.at[0], dst_ref=p_z.at[d], send_sem=pz_send_sem.at[d], recv_sem=pz_recv_sem.at[d],
            device_id=(z_peer[d], tensor), device_id_type=MESH)
        for d in Z_ORDER
    ]
    for copy in pz_copies:
        copy.start()

    for copy in w_copies:
        copy.wait()
    for copy in st_copies:
        copy.wait_recv()
    row16 = lax.broadcasted_iota(jnp.int32, (16, HD), 0) // STEPS

    def project(d, acc):
        source = (tensor - d + NT) % NT
        for h in range(2):
            x = st_all[d, h * 16:(h + 1) * 16, :].astype(F32)
            left = jnp.concatenate([jnp.where(row16 == g, x, 0.0) for g in range(4)], axis=1).astype(BF16)
            weight = jnp.concatenate(
                [kw_buf[source, h * 512:(h + 1) * 512, :], vw_buf[source, h * 512:(h + 1) * 512, :]], axis=1)
            acc = acc + jnp.dot(left, weight, preferred_element_type=F32)
        return acc

    acc = lax.fori_loop(0, NT, project, jnp.zeros((16, 2 * HD), F32))
    acc = acc[:8] + acc[8:]
    acc = acc[:4] + acc[4:]
    padded = jnp.concatenate([acc, jnp.zeros((12, 2 * HD), F32)], axis=0).astype(BF16)
    new_keys = padded[:, :HD]
    new_values = padded[:, HD:]
    s = lax.dot_general(query, new_keys, NT_DIMS, preferred_element_type=F32)
    step = lax.broadcasted_iota(jnp.int32, (ROWS, 16), 0) % STEPS
    other = lax.broadcasted_iota(jnp.int32, (ROWS, 16), 1)
    s = jnp.where(other <= step, s * LOG2E_SCALE, NEG)
    merged_top = jnp.maximum(own_top, jnp.max(s, axis=1, keepdims=True))
    w = jnp.exp2(s - merged_top)
    kept = jnp.exp2(own_top - merged_top)
    merged_total = own_total * kept + jnp.sum(w, axis=1, keepdims=True)
    merged_out = own_out * kept + jnp.dot(w.astype(BF16), new_values, preferred_element_type=F32)

    for copy in pz_copies:
        copy.wait_recv()
    p2_copies = []
    for e in Y_ORDER + (0,):
        picked = p_z[(z - (lender[e] >> 2)) & (NZ - 1)]
        if e == 0:
            p2_recv[0] = picked
        else:
            p2_send[e] = picked
            copy = pltpu.make_async_remote_copy(
                src_ref=p2_send.at[e], dst_ref=p2_recv.at[e], send_sem=p2_send_sem.at[e], recv_sem=p2_recv_sem.at[e],
                device_id=(y_peer[e], tensor), device_id_type=MESH)
            copy.start()
            p2_copies.append(copy)

    for copy in p2_copies:
        copy.wait_recv()
    lent_part = p2_recv[(y - lender[0]) & (NY - 1)].astype(F32)
    coded = lent_part[ROWS:]
    lane16 = lane[:half_rows]
    level = jnp.concatenate([
        jnp.sum(jnp.where(lane16 < 64, coded, 0.0), axis=1, keepdims=True),
        jnp.sum(jnp.where(lane16 < 64, 0.0, coded), axis=1, keepdims=True)], axis=0)
    level = jnp.where(lender[0] >= 0, level, NEG)
    highest = jnp.maximum(merged_top, level)
    kept = jnp.exp2(merged_top - highest)
    added = jnp.exp2(level - highest)
    out_ref[...] = ((merged_out * kept + lent_part[:ROWS] * added) / (merged_total * kept + added)).astype(out_ref.dtype)

    for copy in qz_copies + st_copies + q2_copies + pz_copies + p2_copies:
        copy.wait_send()


def on_device(queries, new_states, key_weight, value_weight, key_pool, value_pool, lengths, page_table):
    hbm = pl.BlockSpec(memory_space=pltpu.HBM)
    dma = pltpu.SemaphoreType.DMA

    def rows_of(x):
        return jnp.transpose(x.reshape(STEPS, GROUP, HD), (1, 0, 2)).reshape(ROWS, HD)

    out = pl.pallas_call(
        kernel,
        out_shape=pltpu.VMEM((ROWS, HD), F32),
        in_specs=[hbm] * 8,
        out_specs=pl.BlockSpec(memory_space=pltpu.VMEM),
        scratch_shapes=[
            pltpu.SMEM((1, 32), jnp.int32),
            pltpu.SMEM((32, SLOTS), jnp.int32),
            pltpu.VMEM((32, SLOTS), jnp.int32),
            pltpu.VMEM((SLOTS, PAGE, HD), BF16),
            pltpu.VMEM((SLOTS, PAGE, HD), BF16),
            pltpu.VMEM((NT, GROUP * HD, HD), BF16),
            pltpu.VMEM((NT, GROUP * HD, HD), BF16),
            pltpu.VMEM((CHUNKS, ROWS, CHUNK * PAGE), F32),
            pltpu.VMEM((ROWS, LENT * PAGE), F32),
            pltpu.VMEM((SLOTS, PAGE), F32),
            pltpu.VMEM((NT, ROWS, HD), BF16),
            pltpu.VMEM((NZ, ROWS, HD), BF16),
            pltpu.VMEM((NY, ROWS, HD), BF16),
            pltpu.VMEM((NY, ROWS, HD), BF16),
            pltpu.VMEM((NZ, ROWS + 16, HD), BF16),
            pltpu.VMEM((NY, ROWS + 16, HD), BF16),
            pltpu.VMEM((NY, ROWS + 16, HD), BF16),
            dma((5,)), dma((CHUNKS,)), dma((CHUNKS,)), dma((2,)),
            dma((NT,)), dma((NT,)), dma((NZ,)), dma((NZ,)), dma((NY,)), dma((NY,)),
            dma((NZ,)), dma((NZ,)), dma((NY,)), dma((NY,)),
        ],
        compiler_params=pltpu.CompilerParams(
            collective_id=0, has_side_effects=True, vmem_limit_bytes=VMEM_BYTES),
    )(
        lengths.reshape(1, -1), page_table, rows_of(queries), rows_of(new_states),
        key_weight.reshape(NT, GROUP * HD, HD), value_weight.reshape(NT, GROUP * HD, HD),
        key_pool, value_pool,
    )
    return (
        jnp.transpose(out.reshape(GROUP, STEPS, HD), (1, 0, 2))
        .reshape(1, STEPS, GROUP * HD)
        .astype(BF16)
    )


def solution(mesh):
    placed = (
        P("inst", None, "tensor"),
        P("inst", None, "tensor"),
        P(None, "tensor"),
        P(None, "tensor"),
        P("inst", None, "tensor"),
        P("inst", None, "tensor"),
        P(),
        P(),
    )
    return jax.shard_map(
        on_device, mesh=mesh, in_specs=placed, out_specs=P("inst", None, "tensor"), check_vma=False
    )
```

time: 35.3 us -> 27 us (0.76)
  local copies, waits for them, and re-layouts: 5.95 us -> 0 us
  Pallas kernels: 28.4 us -> 26.3 us
    unnamed x12 -> x0, local copies, waits for them, and re-layouts: 5.95 us -> none
    pallas_call x1, Pallas kernels: 28.4 us -> 26.3 us  [on_device(): pl.pallas_call(kernel, out_shape=pltpu.VMEM((ROWS, HD), F32), in_specs=[h...]
where the time goes in v2:
time: 27 us; the launch traced here: 26.9 us
  Pallas kernels  26.3 us (97%)
  other arithmetic  0.6 us (2%)
    pallas_call x1, Pallas kernels, on_device(): pl.pallas_call(kernel, out_shape=pltpu.VMEM((ROWS, HD), F32), in_specs=[h...  26.3 us
    convert_element_type x1, other arithmetic, on_device(): return jnp.transpose(out.reshape(GROUP, STEPS, HD), (1, 0, 2)).reshape(1,...  0.6 us

profile of v2, /device:TPU:4, one launch (start us, length us, event | category | flops | bytes accessed | tf_op | source)
XLA Modules:
  0.0 26.9 jit_solution(1327436293883314703)
XLA Ops:
  0.0 26.3 %shard_map.82 = f32[32,128]{1,0:T(8,128)S(1)} custom-call(s32[1,32]{1,0:T(1,128)} %bitcast.22, s32[32,64]{1,0:T(8,128)} %tab_hbm.1, bf16[32,128]{1,0:T(8,128)(2,1)} %bitcast.20, bf16[32,128]{1,0:T(8,128)(2,1)} %bitcast.21, bf16[8,1024,128]{2,1,0:T(8,128)(2,1)} %bitcast.18, bf16[8,1024,128]{2,1,0:T(8,128)(2,1)} %bitcast.19, bf16[64,256,128]{2,1,0:T(8,128)(2,1)} %k_hbm.1, ...), custom_call_target="tpu_custom_call" | custom-call | tf_op jit(solution)/shard_map/pallas_call | solution.py:307
  26.3 0.6 %convert_element_type.20 = bf16[32,128]{1,0:T(8,128)(2,1)} convert(f32[32,128]{1,0:T(8,128)S(1)} %shard_map.82) | non-fusion elementwise | flops 4096 | bytes 24576 | tf_op jit(solution)/shard_map/convert_element_type | solution.py:344

commit v3 on v2

--- a/solution.py
+++ b/solution.py
@@ -15,6 +15,8 @@
 SLOTS = 64
 CHUNK = 8
 CHUNKS = SLOTS // CHUNK
+PARTS = 4
+PART = SLOTS // PARTS
 LENT = 16
 NY = 4
 NZ = 8
@@ -31,35 +33,56 @@
 NT_DIMS = (((1,), (1,)), ((), ()))
 
 
+def remote_copy(src, dst, send_sem, recv_sem, target):
+    return pltpu.make_async_remote_copy(
+        src_ref=src, dst_ref=dst, send_sem=send_sem, recv_sem=recv_sem, device_id=target, device_id_type=MESH)
+
+
+def lanes_sum(w):
+    total = w[:, :HD]
+    for b in range(1, w.shape[1] // HD):
+        total = total + w[:, b * HD:(b + 1) * HD]
+    return total
+
+
 def kernel(
     len_hbm, tab_hbm, q_hbm, st_hbm, kw_hbm, vw_hbm, k_hbm, v_hbm,
     out_ref,
     len_smem, tab_smem, tab_ref, k_buf, v_buf, kw_buf, vw_buf, s_buf, guest_buf, bias_buf,
-    st_all, q_z, q2_send, q2_recv, p_z, p2_send, p2_recv,
-    small_sem, k_sem, v_sem, w_sem,
-    st_send_sem, st_recv_sem, qz_send_sem, qz_recv_sem, q2_send_sem, q2_recv_sem,
-    pz_send_sem, pz_recv_sem, p2_send_sem, p2_recv_sem,
+    st_all, q_own, q_relay_even, q_relay_odd, q_send, q_recv, p_own, p_relay_even, p_relay_odd, p_send, p_recv,
+    small_sem, k_sem, v_sem, w_sem, st_send_sem, st_recv_sem,
+    q1_send_sem, q1_recv_sem, q2_send_sem, q2_recv_sem,
+    p1_send_sem, p1_recv_sem, p2_send_sem, p2_recv_sem,
 ):
     inst = lax.axis_index("inst")
     tensor = lax.axis_index("tensor")
     z = inst // NY
     y = inst % NY
+    odd = tensor % 2
+    even_t = tensor - odd
+    odd_t = even_t + 1
+    is_relay = odd == 1
     z_peer = [((z + d) % NZ) * NY + y for d in range(NZ)]
     y_peer = [z * NY + (y + e) % NY for e in range(NY)]
     t_peer = [(tensor + d) % NT for d in range(NT)]
 
     barrier = pltpu.get_barrier_semaphore()
-    for d in Z_ORDER:
-        pl.semaphore_signal(barrier, inc=1, device_id=(z_peer[d], tensor), device_id_type=MESH)
+
+    @pl.when(is_relay)
+    def _():
+        for d in Z_ORDER:
+            pl.semaphore_signal(barrier, inc=1, device_id=(z_peer[d], even_t), device_id_type=MESH)
+            pl.semaphore_signal(barrier, inc=1, device_id=(z_peer[d], odd_t), device_id_type=MESH)
+
     for e in Y_ORDER:
-        pl.semaphore_signal(barrier, inc=1, device_id=(y_peer[e], tensor), device_id_type=MESH)
+        pl.semaphore_signal(barrier, inc=1, device_id=(y_peer[e], odd_t), device_id_type=MESH)
     for d in T_ORDER:
         pl.semaphore_signal(barrier, inc=1, device_id=(inst, t_peer[d]), device_id_type=MESH)
 
     small_copies = [
-        pltpu.make_async_copy(tab_hbm, tab_ref, small_sem.at[0]),
-        pltpu.make_async_copy(q_hbm, q_z.at[0], small_sem.at[1]),
-        pltpu.make_async_copy(st_hbm, st_all.at[0], small_sem.at[2]),
+        pltpu.make_async_copy(q_hbm, q_own, small_sem.at[0]),
+        pltpu.make_async_copy(st_hbm, st_all.at[0], small_sem.at[1]),
+        pltpu.make_async_copy(tab_hbm, tab_ref, small_sem.at[2]),
         pltpu.make_async_copy(len_hbm, len_smem, small_sem.at[3]),
         pltpu.make_async_copy(tab_hbm, tab_smem, small_sem.at[4]),
     ]
@@ -67,46 +90,98 @@
         copy.start()
 
     def k_copy(c):
-        part = pl.ds(c * CHUNK, CHUNK)
+        part = pl.ds(c * PART, PART)
         return pltpu.make_async_copy(k_hbm.at[part], k_buf.at[part], k_sem.at[c])
 
     def v_copy(c):
-        part = pl.ds(c * CHUNK, CHUNK)
+        part = pl.ds(c * PART, PART)
         return pltpu.make_async_copy(v_hbm.at[part], v_buf.at[part], v_sem.at[c])
 
-    for c in range(CHUNKS):
-        k_copy(c).start()
-    for c in range(CHUNKS):
-        v_copy(c).start()
     w_copies = [
         pltpu.make_async_copy(kw_hbm, kw_buf, w_sem.at[0]),
         pltpu.make_async_copy(vw_hbm, vw_buf, w_sem.at[1]),
     ]
+    for c in range(PARTS):
+        k_copy(c).start()
+    for c in range(PARTS):
+        v_copy(c).start()
     for copy in w_copies:
         copy.start()
 
+    small_copies[0].wait()
     small_copies[1].wait()
-    small_copies[2].wait()
-    pl.semaphore_wait(barrier, NZ + NY + NT - 3)
-
-    qz_copies = [
-        pltpu.make_async_remote_copy(
-            src_ref=q_z.at[0], dst_ref=q_z.at[d], send_sem=qz_send_sem.at[d], recv_sem=qz_recv_sem.at[d],
-            device_id=(z_peer[d], tensor), device_id_type=MESH)
-        for d in Z_ORDER
-    ]
+    query = q_own[...]
+    q_relay_odd[0] = query
+    pl.semaphore_wait(barrier, NZ + NT - 2 + (NY + NY - 2) * odd)
+
+    def relay_copy(own, relay, d, p, send_sem, recv_sem):
+        return remote_copy(own, relay[p].at[d], send_sem.at[d], recv_sem.at[p, d], (z_peer[d], odd_t))
+
+    def to_relays(own, relay, send_sem, recv_sem):
+        @pl.when(is_relay)
+        def _():
+            for d in Z_ORDER:
+                relay_copy(own, relay, d, 1, send_sem, recv_sem).start()
+
+        @pl.when(jnp.logical_not(is_relay))
+        def _():
+            for d in Z_ORDER + (0,):
+                relay_copy(own, relay, d, 0, send_sem, recv_sem).start()
+
+    def to_relays_done(own, relay, send_sem, recv_sem):
+        for d in Z_ORDER:
+            relay_copy(own, relay, d, 0, send_sem, recv_sem).wait_send()
+
+        @pl.when(jnp.logical_not(is_relay))
+        def _():
+            relay_copy(own, relay, 0, 0, send_sem, recv_sem).wait_send()
+
+    def relayed(relay, source, sent, received, arrive_sem, send_sem, recv_sem):
+        @pl.when(is_relay)
+        def _():
+            for p in (1, 0):
+                for d in Z_ORDER + (0,) * (1 - p):
+                    relay_copy(sent.at[p, 0], relay, d, p, arrive_sem.at[p], arrive_sem).wait_recv()
+                for e in Y_ORDER + (0,):
+                    picked = relay[p][source[e]]
+                    if p == 1 and e == 0:
+                        received[0] = picked
+                    else:
+                        sent[p, e] = picked
+                        remote_copy(
+                            sent.at[p, e], received.at[e], send_sem.at[p, e], recv_sem.at[e], (y_peer[e], even_t + p)
+                        ).start()
+
+    def relay_done(sent, received, send_sem, recv_sem):
+        for p in range(2):
+            for e in Y_ORDER + (0,) * (1 - p):
+                remote_copy(
+                    sent.at[p, e], received.at[e], send_sem.at[p, e], recv_sem.at[e], (y_peer[e], even_t + p)
+                ).wait_send()
+
+    def arrived(received, recv_sem):
+        for e in Y_ORDER:
+            remote_copy(
+                received.at[e], received.at[e], recv_sem.at[e], recv_sem.at[e], (y_peer[e], odd_t)
+            ).wait_recv()
+
+        @pl.when(jnp.logical_not(is_relay))
+        def _():
+            remote_copy(
+                received.at[0], received.at[0], recv_sem.at[0], recv_sem.at[0], (inst, odd_t)
+            ).wait_recv()
+
+    q_relay = (q_relay_even, q_relay_odd)
+    to_relays(q_own, q_relay, q1_send_sem, q1_recv_sem)
     st_copies = [
-        pltpu.make_async_remote_copy(
-            src_ref=st_all.at[0], dst_ref=st_all.at[d], send_sem=st_send_sem.at[d], recv_sem=st_recv_sem.at[d],
-            device_id=(inst, t_peer[d]), device_id_type=MESH)
+        remote_copy(st_all.at[0], st_all.at[d], st_send_sem.at[d], st_recv_sem.at[d], (inst, t_peer[d]))
         for d in T_ORDER
     ]
-    for copy in qz_copies + st_copies:
+    for copy in st_copies:
         copy.start()
 
-    small_copies[0].wait()
-    small_copies[3].wait()
-    small_copies[4].wait()
+    for copy in small_copies[2:]:
+        copy.wait()
     table = tab_ref[...]
     holder = table >> 6
     row_id = lax.broadcasted_iota(jnp.int32, table.shape, 0)
@@ -139,10 +214,7 @@
         slots.append(jnp.clip(tab_smem[guest_row, page] - inst * SLOTS, 0, SLOTS - 1))
         limits.append(jnp.where(i < guest_pages, guest_length - page * PAGE, 0))
 
-    query = q_z[0]
-
     def scores_chunk(c, top):
-        k_copy(c).wait()
         for p in range(CHUNK):
             slot = c * CHUNK + p
             s = lax.dot_general(query, k_buf[slot], NT_DIMS, preferred_element_type=F32)
@@ -151,15 +223,8 @@
             top = jnp.maximum(top, jnp.maximum(s[:, :HD], s[:, HD:]))
         return top
 
-    def lanes_sum(w):
-        total = w[:, :HD]
-        for b in range(1, w.shape[1] // HD):
-            total = total + w[:, b * HD:(b + 1) * HD]
-        return total
-
     def values_chunk(c, carry):
         total, numerator = carry
-        v_copy(c).wait()
         half = CHUNK // 2
         for h in range(2):
             s = s_buf[c, :, h * half * PAGE:(h + 1) * half * PAGE]
@@ -169,34 +234,26 @@
             numerator = numerator + jnp.dot(w.astype(BF16), v, preferred_element_type=F32)
         return total, numerator
 
+    per_part = CHUNKS // PARTS
     top = jnp.full((ROWS, HD), NEG, F32)
-    top = lax.fori_loop(0, CHUNKS, scores_chunk, top)
-
-    for copy in qz_copies:
-        copy.wait_recv()
-    q2_copies = []
-    for e in Y_ORDER + (0,):
-        picked = q_z[(z - (guest_code[e] >> 8)) & (NZ - 1)]
-        if e == 0:
-            q2_recv[0] = picked
-        else:
-            q2_send[e] = picked
-            copy = pltpu.make_async_remote_copy(
-                src_ref=q2_send.at[e], dst_ref=q2_recv.at[e], send_sem=q2_send_sem.at[e], recv_sem=q2_recv_sem.at[e],
-                device_id=(y_peer[e], tensor), device_id_type=MESH)
-            copy.start()
-            q2_copies.append(copy)
-
+    for c in range(PARTS):
+        k_copy(c).wait()
+        top = lax.fori_loop(c * per_part, (c + 1) * per_part, scores_chunk, top)
     own_top = jnp.max(top, axis=1, keepdims=True) * LOG2E_SCALE
 
+    relayed(
+        q_relay, [(z - (guest_code[e] >> 8)) & (NZ - 1) for e in range(NY)], q_send, q_recv,
+        q1_recv_sem, q2_send_sem, q2_recv_sem)
+
     carry = (jnp.zeros((ROWS, HD), F32), jnp.zeros((ROWS, HD), F32))
-    carry = lax.fori_loop(0, CHUNKS, values_chunk, carry)
+    for c in range(PARTS):
+        v_copy(c).wait()
+        carry = lax.fori_loop(c * per_part, (c + 1) * per_part, values_chunk, carry)
     total, own_out = carry
     own_total = jnp.sum(total, axis=1, keepdims=True)
 
-    for copy in q2_copies:
-        copy.wait_recv()
-    guest_query = q2_recv[(y - guest) & (NY - 1)]
+    arrived(q_recv, q2_recv_sem)
+    guest_query = q_recv[(y - guest) & (NY - 1)]
     guest_top = jnp.full((ROWS, HD), NEG, F32)
     for i in range(LENT):
         s = lax.dot_general(guest_query, k_buf[slots[i]], NT_DIMS, preferred_element_type=F32)
@@ -221,16 +278,11 @@
     coded = jnp.where(place == 0, high, jnp.where(place == 1, middle, jnp.where(place == 2, low, 0.0)))
     half_rows = ROWS // 2
     coded = jnp.where(lane[:half_rows] < 64, coded[:half_rows], coded[half_rows:])
-    p_z[0, :ROWS, :] = (guest_out / guest_total).astype(BF16)
-    p_z[0, ROWS:, :] = coded.astype(BF16)
-    pz_copies = [
-        pltpu.make_async_remote_copy(
-            src_ref=p_z.at[0], dst_ref=p_z.at[d], send_sem=pz_send_sem.at[d], recv_sem=pz_recv_sem.at[d],
-            device_id=(z_peer[d], tensor), device_id_type=MESH)
-        for d in Z_ORDER
-    ]
-    for copy in pz_copies:
-        copy.start()
+    result = jnp.concatenate([guest_out / guest_total, coded], axis=0).astype(BF16)
+    p_own[...] = result
+    p_relay = (p_relay_even, p_relay_odd)
+    to_relays(p_own, p_relay, p1_send_sem, p1_recv_sem)
+    p_relay_odd[0] = result
 
     for copy in w_copies:
         copy.wait()
@@ -264,24 +316,11 @@
     merged_total = own_total * kept + jnp.sum(w, axis=1, keepdims=True)
     merged_out = own_out * kept + jnp.dot(w.astype(BF16), new_values, preferred_element_type=F32)
 
-    for copy in pz_copies:
-        copy.wait_recv()
-    p2_copies = []
-    for e in Y_ORDER + (0,):
-        picked = p_z[(z - (lender[e] >> 2)) & (NZ - 1)]
-        if e == 0:
-            p2_recv[0] = picked
-        else:
-            p2_send[e] = picked
-            copy = pltpu.make_async_remote_copy(
-                src_ref=p2_send.at[e], dst_ref=p2_recv.at[e], send_sem=p2_send_sem.at[e], recv_sem=p2_recv_sem.at[e],
-                device_id=(y_peer[e], tensor), device_id_type=MESH)
-            copy.start()
-            p2_copies.append(copy)
-
-    for copy in p2_copies:
-        copy.wait_recv()
-    lent_part = p2_recv[(y - lender[0]) & (NY - 1)].astype(F32)
+    relayed(
+        p_relay, [(z - (lender[e] >> 2)) & (NZ - 1) for e in range(NY)], p_send, p_recv,
+        p1_recv_sem, p2_send_sem, p2_recv_sem)
+    arrived(p_recv, p2_recv_sem)
+    lent_part = p_recv[(y - lender[0]) & (NY - 1)].astype(F32)
     coded = lent_part[ROWS:]
     lane16 = lane[:half_rows]
     level = jnp.concatenate([
@@ -291,10 +330,17 @@
     highest = jnp.maximum(merged_top, level)
     kept = jnp.exp2(merged_top - highest)
     added = jnp.exp2(level - highest)
-    out_ref[...] = ((merged_out * kept + lent_part[:ROWS] * added) / (merged_total * kept + added)).astype(out_ref.dtype)
-
-    for copy in qz_copies + st_copies + q2_copies + pz_copies + p2_copies:
+    out_ref[...] = (merged_out * kept + lent_part[:ROWS] * added) / (merged_total * kept + added)
+
+    for copy in st_copies:
         copy.wait_send()
+    to_relays_done(q_own, q_relay, q1_send_sem, q1_recv_sem)
+    to_relays_done(p_own, p_relay, p1_send_sem, p1_recv_sem)
+
+    @pl.when(is_relay)
+    def _():
+        relay_done(q_send, q_recv, q2_send_sem, q2_recv_sem)
+        relay_done(p_send, p_recv, p2_send_sem, p2_recv_sem)
 
 
 def on_device(queries, new_states, key_weight, value_weight, key_pool, value_pool, lengths, page_table):
@@ -321,15 +367,19 @@
             pltpu.VMEM((ROWS, LENT * PAGE), F32),
             pltpu.VMEM((SLOTS, PAGE), F32),
             pltpu.VMEM((NT, ROWS, HD), BF16),
+            pltpu.VMEM((ROWS, HD), BF16),
             pltpu.VMEM((NZ, ROWS, HD), BF16),
+            pltpu.VMEM((NZ, ROWS, HD), BF16),
+            pltpu.VMEM((2, NY, ROWS, HD), BF16),
             pltpu.VMEM((NY, ROWS, HD), BF16),
-            pltpu.VMEM((NY, ROWS, HD), BF16),
+            pltpu.VMEM((ROWS + 16, HD), BF16),
             pltpu.VMEM((NZ, ROWS + 16, HD), BF16),
+            pltpu.VMEM((NZ, ROWS + 16, HD), BF16),
+            pltpu.VMEM((2, NY, ROWS + 16, HD), BF16),
             pltpu.VMEM((NY, ROWS + 16, HD), BF16),
-            pltpu.VMEM((NY, ROWS + 16, HD), BF16),
-            dma((5,)), dma((CHUNKS,)), dma((CHUNKS,)), dma((2,)),
-            dma((NT,)), dma((NT,)), dma((NZ,)), dma((NZ,)), dma((NY,)), dma((NY,)),
-            dma((NZ,)), dma((NZ,)), dma((NY,)), dma((NY,)),
+            dma((5,)), dma((PARTS,)), dma((PARTS,)), dma((2,)), dma((NT,)), dma((NT,)),
+            dma((NZ,)), dma((2, NZ)), dma((2, NY)), dma((NY,)),
+            dma((NZ,)), dma((2, NZ)), dma((2, NY)), dma((NY,)),
         ],
         compiler_params=pltpu.CompilerParams(
             collective_id=0, has_side_effects=True, vmem_limit_bytes=VMEM_BYTES),

time: 27 us -> 25.1 us (0.930)
  Pallas kernels: 26.3 us -> 24.3 us
    pallas_call x1, Pallas kernels: 26.3 us -> 24.3 us  [on_device(): pl.pallas_call(kernel, out_shape=pltpu.VMEM((ROWS, HD), F32), in_specs=[h...]
where the time goes in v3:
time: 25.1 us; the launch traced here: 24.9 us
  Pallas kernels  24.3 us (97%)
  other arithmetic  0.6 us (2%)
    pallas_call x1, Pallas kernels, on_device(): pl.pallas_call(kernel, out_shape=pltpu.VMEM((ROWS, HD), F32), in_specs=[h...  24.3 us
    convert_element_type x1, other arithmetic, on_device(): return jnp.transpose(out.reshape(GROUP, STEPS, HD), (1, 0, 2)).reshape(1,...  0.6 us

profile of v3, /device:TPU:4, one launch (start us, length us, event | category | flops | bytes accessed | tf_op | source)
XLA Modules:
  0.0 24.9 jit_solution(5868782163760049828)
XLA Ops:
  0.0 24.3 %shard_map.82 = f32[32,128]{1,0:T(8,128)S(1)} custom-call(s32[1,32]{1,0:T(1,128)} %bitcast.22, s32[32,64]{1,0:T(8,128)} %tab_hbm.1, bf16[32,128]{1,0:T(8,128)(2,1)} %bitcast.20, bf16[32,128]{1,0:T(8,128)(2,1)} %bitcast.21, bf16[8,1024,128]{2,1,0:T(8,128)(2,1)} %bitcast.18, bf16[8,1024,128]{2,1,0:T(8,128)(2,1)} %bitcast.19, bf16[64,256,128]{2,1,0:T(8,128)(2,1)} %k_hbm.1, ...), custom_call_target="tpu_custom_call" | custom-call | tf_op jit(solution)/shard_map/pallas_call | solution.py:353
  24.3 0.6 %convert_element_type.20 = bf16[32,128]{1,0:T(8,128)(2,1)} convert(f32[32,128]{1,0:T(8,128)S(1)} %shard_map.82) | non-fusion elementwise | flops 4096 | bytes 24576 | tf_op jit(solution)/shard_map/convert_element_type | solution.py:394

commit v4 on v3

--- a/solution.py
+++ b/solution.py
@@ -26,6 +26,8 @@
 Z_ORDER = (4, 3, 5, 2, 6, 1, 7)
 Y_ORDER = (2, 1, 3)
 T_ORDER = (4, 5, 3, 2, 6, 7, 1)
+R_ORDER = (4, 3, 5, 2, 6, 1, 7)
+STRAIGHT = ((4, 2, 0),)
 LOG2E_SCALE = math.log2(math.e) / math.sqrt(HD)
 F32 = jnp.float32
 BF16 = jnp.bfloat16
@@ -49,10 +51,10 @@
     len_hbm, tab_hbm, q_hbm, st_hbm, kw_hbm, vw_hbm, k_hbm, v_hbm,
     out_ref,
     len_smem, tab_smem, tab_ref, k_buf, v_buf, kw_buf, vw_buf, s_buf, guest_buf, bias_buf,
-    st_all, q_own, q_relay_even, q_relay_odd, q_send, q_recv, p_own, p_relay_even, p_relay_odd, p_send, p_recv,
+    st_all, q_own, q_relay_even, q_relay_odd, q_send, q_recv, p_own, p_near_even, p_near_odd, p_far_even, p_far_odd, p_send, p_recv, p_straight,
     small_sem, k_sem, v_sem, w_sem, st_send_sem, st_recv_sem,
     q1_send_sem, q1_recv_sem, q2_send_sem, q2_recv_sem,
-    p1_send_sem, p1_recv_sem, p2_send_sem, p2_recv_sem,
+    p1_send_sem, p1_recv_sem, p2_send_sem, p2_recv_sem, ps_send_sem, ps_recv_sem,
 ):
     inst = lax.axis_index("inst")
     tensor = lax.axis_index("tensor")
@@ -280,9 +282,38 @@
     coded = jnp.where(lane[:half_rows] < 64, coded[:half_rows], coded[half_rows:])
     result = jnp.concatenate([guest_out / guest_total, coded], axis=0).astype(BF16)
     p_own[...] = result
-    p_relay = (p_relay_even, p_relay_odd)
-    to_relays(p_own, p_relay, p1_send_sem, p1_recv_sem)
-    p_relay_odd[0] = result
+    p_near, p_far = (p_near_even, p_near_odd), (p_far_even, p_far_odd)
+
+    def p_slot(p, d):
+        if d == 4:
+            return p_far[p].at[0]
+        return p_near[p].at[d if d < 4 else d - 1]
+
+    def p1_copy(p, d):
+        return remote_copy(p_own, p_slot(p, d), p1_send_sem.at[d], p1_recv_sem.at[p, d], (z_peer[d], odd_t))
+
+    straight_copies = [
+        remote_copy(
+            p_own, p_straight.at[k], ps_send_sem.at[k], ps_recv_sem.at[k],
+            (((z + dz) % NZ) * NY + (y + dy) % NY, tensor))
+        for dz, dy, k in STRAIGHT
+    ]
+
+    @pl.when(is_relay)
+    def _():
+        p1_copy(1, 4).start()
+        straight_copies[0].start()
+        for d in R_ORDER[1:]:
+            p1_copy(1, d).start()
+
+    @pl.when(jnp.logical_not(is_relay))
+    def _():
+        p1_copy(0, 4).start()
+        straight_copies[0].start()
+        for d in R_ORDER[1:] + (0,):
+            p1_copy(0, d).start()
+
+    p_near_odd[0] = result
 
     for copy in w_copies:
         copy.wait()
@@ -316,11 +347,33 @@
     merged_total = own_total * kept + jnp.sum(w, axis=1, keepdims=True)
     merged_out = own_out * kept + jnp.dot(w.astype(BF16), new_values, preferred_element_type=F32)
 
-    relayed(
-        p_relay, [(z - (lender[e] >> 2)) & (NZ - 1) for e in range(NY)], p_send, p_recv,
-        p1_recv_sem, p2_send_sem, p2_recv_sem)
+    @pl.when(is_relay)
+    def _():
+        for p in (1, 0):
+            for group, targets in (((3, 5, 2, 6, 1, 7), (2,)), ((4,), (1, 3, 0))):
+                for d in group + ((0,) if p == 0 and 2 in targets else ()):
+                    p1_copy(p, d).wait_recv()
+                for e in targets:
+                    source = (z - (lender[e] >> 2)) & (NZ - 1)
+                    picked = p_near[p][jnp.where(source <= 3, source, source - 1)]
+                    if e != 2:
+                        picked = lax.select(source == 4, p_far[p][0], picked)
+                    if p == 1 and e == 0:
+                        p_recv[0] = picked
+                    else:
+                        p_send[p, e] = picked
+                        remote_copy(
+                            p_send.at[p, e], p_recv.at[e], p2_send_sem.at[p, e], p2_recv_sem.at[e],
+                            (y_peer[e], even_t + p)
+                        ).start()
+
     arrived(p_recv, p2_recv_sem)
-    lent_part = p_recv[(y - lender[0]) & (NY - 1)].astype(F32)
+    for copy in straight_copies:
+        copy.wait_recv()
+    from_z = (z - (lender[0] >> 2)) & (NZ - 1)
+    from_y = (y - lender[0]) & (NY - 1)
+    straight = (from_z == 4) & (from_y == 2)
+    lent_part = lax.select(straight, p_straight[0], p_recv[from_y]).astype(F32)
     coded = lent_part[ROWS:]
     lane16 = lane[:half_rows]
     level = jnp.concatenate([
@@ -335,7 +388,15 @@
     for copy in st_copies:
         copy.wait_send()
     to_relays_done(q_own, q_relay, q1_send_sem, q1_recv_sem)
-    to_relays_done(p_own, p_relay, p1_send_sem, p1_recv_sem)
+    for d in Z_ORDER:
+        p1_copy(0, d).wait_send()
+
+    @pl.when(jnp.logical_not(is_relay))
+    def _():
+        p1_copy(0, 0).wait_send()
+
+    for copy in straight_copies:
+        copy.wait_send()
 
     @pl.when(is_relay)
     def _():
@@ -373,13 +434,16 @@
             pltpu.VMEM((2, NY, ROWS, HD), BF16),
             pltpu.VMEM((NY, ROWS, HD), BF16),
             pltpu.VMEM((ROWS + 16, HD), BF16),
-            pltpu.VMEM((NZ, ROWS + 16, HD), BF16),
-            pltpu.VMEM((NZ, ROWS + 16, HD), BF16),
+            pltpu.VMEM((7, ROWS + 16, HD), BF16),
+            pltpu.VMEM((7, ROWS + 16, HD), BF16),
+            pltpu.VMEM((1, ROWS + 16, HD), BF16),
+            pltpu.VMEM((1, ROWS + 16, HD), BF16),
             pltpu.VMEM((2, NY, ROWS + 16, HD), BF16),
             pltpu.VMEM((NY, ROWS + 16, HD), BF16),
+            pltpu.VMEM((1, ROWS + 16, HD), BF16),
             dma((5,)), dma((PARTS,)), dma((PARTS,)), dma((2,)), dma((NT,)), dma((NT,)),
             dma((NZ,)), dma((2, NZ)), dma((2, NY)), dma((NY,)),
-            dma((NZ,)), dma((2, NZ)), dma((2, NY)), dma((NY,)),
+            dma((NZ,)), dma((2, NZ)), dma((2, NY)), dma((NY,)), dma((1,)), dma((1,)),
         ],
         compiler_params=pltpu.CompilerParams(
             collective_id=0, has_side_effects=True, vmem_limit_bytes=VMEM_BYTES),

time: 25.1 us -> 25.2 us (level)
  no operation moved by 1% of the time
where the time goes in v4:
time: 25.2 us; the launch traced here: 25.1 us
  Pallas kernels  24.4 us (97%)
  other arithmetic  0.6 us (2%)
    pallas_call x1, Pallas kernels, on_device(): pl.pallas_call(kernel, out_shape=pltpu.VMEM((ROWS, HD), F32), in_specs=[h...  24.4 us
    convert_element_type x1, other arithmetic, on_device(): return jnp.transpose(out.reshape(GROUP, STEPS, HD), (1, 0, 2)).reshape(1,...  0.6 us

profile of v4, /device:TPU:4, one launch (start us, length us, event | category | flops | bytes accessed | tf_op | source)
XLA Modules:
  0.0 25.1 jit_solution(110200039610914045)
XLA Ops:
  0.0 24.4 %shard_map.82 = f32[32,128]{1,0:T(8,128)S(1)} custom-call(s32[1,32]{1,0:T(1,128)} %bitcast.22, s32[32,64]{1,0:T(8,128)} %tab_hbm.1, bf16[32,128]{1,0:T(8,128)(2,1)} %bitcast.20, bf16[32,128]{1,0:T(8,128)(2,1)} %bitcast.21, bf16[8,1024,128]{2,1,0:T(8,128)(2,1)} %bitcast.18, bf16[8,1024,128]{2,1,0:T(8,128)(2,1)} %bitcast.19, bf16[64,256,128]{2,1,0:T(8,128)(2,1)} %k_hbm.1, ...), custom_call_target="tpu_custom_call" | custom-call | tf_op jit(solution)/shard_map/pallas_call | solution.py:414
  24.4 0.6 %convert_element_type.20 = bf16[32,128]{1,0:T(8,128)(2,1)} convert(f32[32,128]{1,0:T(8,128)S(1)} %shard_map.82) | non-fusion elementwise | flops 4096 | bytes 24576 | tf_op jit(solution)/shard_map/convert_element_type | solution.py:458

commit v5 on v3

v5 whole, which is shorter than its diff:
```python
import math

import jax
import jax.numpy as jnp
from jax import lax
from jax.experimental import pallas as pl
from jax.experimental.pallas import tpu as pltpu
from jax.sharding import PartitionSpec as P

HD = 128
STEPS = 4
GROUP = 8
ROWS = STEPS * GROUP
PAGE = 256
SLOTS = 64
CHUNK = 8
CHUNKS = SLOTS // CHUNK
PARTS = 4
PART = SLOTS // PARTS
LENT = 16
NY = 4
NZ = 8
NT = 8
EARLY = 2
HOMES = (0, 1)
GUESTS = 3
FIRST_ORDER = (0, 1)
NEG = -1e30
VMEM_BYTES = 60 * 1024 * 1024
Z_ORDER = (4, 3, 5, 2, 6, 1, 7)
Y_ORDER = (2, 1, 3)
T_ORDER = (4, 5, 3, 2, 6, 7, 1)
LOG2E_SCALE = math.log2(math.e) / math.sqrt(HD)
F32 = jnp.float32
BF16 = jnp.bfloat16
MESH = pl.DeviceIdType.MESH
NT_DIMS = (((1,), (1,)), ((), ()))


def remote_copy(src, dst, send_sem, recv_sem, target):
    return pltpu.make_async_remote_copy(
        src_ref=src, dst_ref=dst, send_sem=send_sem, recv_sem=recv_sem, device_id=target, device_id_type=MESH)


def lanes_sum(w):
    total = w[:, :HD]
    for b in range(1, w.shape[1] // HD):
        total = total + w[:, b * HD:(b + 1) * HD]
    return total


def kernel(
    len_hbm, tab_hbm, q_hbm, st_hbm, kw_hbm, vw_hbm, k_hbm, v_hbm,
    out_ref,
    len_smem, tab_smem, tab_ref, k_buf, v_buf, kw_buf, vw_buf, s_buf, guest_buf, bias_buf, st_all,
    q_own, q_row_even, q_row_odd, q_late_even, q_late_odd, q_send_first, q_send_second, q_recv_first, q_recv_second,
    p_own_first, p_own_second, p_relay_even, p_relay_odd, p_send, p_recv,
    small_sem, k_sem, v_sem, w_sem, st_send_sem, st_recv_sem, ready_sem, plane_sem, go_sem,
    q1_send_sem, q1_row_sem, q1_late_sem, qa_send_sem, qa_recv_sem, qb_send_sem, qb_recv_sem,
    p1_send_sem, p1_recv_sem, p2_send_sem, p2_recv_sem,
):
    inst = lax.axis_index("inst")
    tensor = lax.axis_index("tensor")
    z = inst // NY
    y = inst % NY
    odd = tensor % 2
    even_t = tensor - odd
    odd_t = even_t + 1
    is_relay = odd == 1
    is_even = odd == 0
    early = z < EARLY
    late = z >= EARLY
    early_relay = early & is_relay
    home_relay = is_relay & ((z == HOMES[0]) | (z == HOMES[1]))
    row = jnp.minimum(z, EARLY - 1)
    home_place = jnp.where(z == HOMES[0], 0, 1)
    home_row = jnp.where(z >= 5, HOMES[0], HOMES[1])
    guests_from = jnp.where(z == HOMES[0], 5, 2)

    def at(zz, yy):
        return zz * NY + yy

    z_peer = [at((z + d) % NZ, y) for d in range(NZ)]
    ys = [(y + e) % NY for e in range(NY)]
    y_peer = [at(z, ys[e]) for e in range(NY)]
    t_peer = [(tensor + d) % NT for d in range(NT)]

    barrier = pltpu.get_barrier_semaphore()

    def greet(where, which):
        pl.semaphore_signal(barrier, inc=1, device_id=(where, which), device_id_type=MESH)

    @pl.when(early_relay)
    def _():
        for zz in range(NZ - 1, EARLY - 1, -1):
            greet(at(zz, y), even_t)
            greet(at(zz, y), odd_t)

    @pl.when(home_relay)
    def _():
        for j in range(GUESTS):
            for e in Y_ORDER:
                greet(at(guests_from + j, ys[e]), even_t)
                greet(at(guests_from + j, ys[e]), odd_t)

    @pl.when(early)
    def _():
        for c in range(1, EARLY):
            greet(at((z + c) % EARLY, y), odd_t)
        for d in T_ORDER:
            greet(inst, t_peer[d])

    @pl.when(early_relay)
    def _():
        for e in Y_ORDER:
            greet(y_peer[e], even_t)
            greet(y_peer[e], odd_t)

    small_copies = [
        pltpu.make_async_copy(q_hbm, q_own, small_sem.at[0]),
        pltpu.make_async_copy(st_hbm, st_all.at[0], small_sem.at[1]),
        pltpu.make_async_copy(tab_hbm, tab_ref, small_sem.at[2]),
        pltpu.make_async_copy(len_hbm, len_smem, small_sem.at[3]),
        pltpu.make_async_copy(tab_hbm, tab_smem, small_sem.at[4]),
    ]
    for copy in small_copies:
        copy.start()

    def k_copy(c):
        part = pl.ds(c * PART, PART)
        return pltpu.make_async_copy(k_hbm.at[part], k_buf.at[part], k_sem.at[c])

    def v_copy(c):
        part = pl.ds(c * PART, PART)
        return pltpu.make_async_copy(v_hbm.at[part], v_buf.at[part], v_sem.at[c])

    w_copies = [
        pltpu.make_async_copy(kw_hbm, kw_buf, w_sem.at[0]),
        pltpu.make_async_copy(vw_hbm, vw_buf, w_sem.at[1]),
    ]

    pl.semaphore_wait(barrier, jnp.where(late, EARLY + NY - 1, jnp.where(is_relay, NY - 1 + 2 * (EARLY - 1) + NT - 1, NY + NT - 2)))

    @pl.when(late)
    def _():
        for c in range(EARLY):
            pl.semaphore_signal(
                ready_sem, inc=1, device_id=(at((z + c) % EARLY, y), odd_t), device_id_type=MESH)

    small_copies[0].wait()

    def q1_copy(place, e, target):
        buffer, slot, sem = place
        return remote_copy(q_own, buffer.at[slot], q1_send_sem.at[e], sem.at[slot], (target, odd_t))

    def q1_row(p, e):
        return q1_copy(((q_row_even, q_row_odd)[p], e, q1_row_sem.at[p]), e, y_peer[e])

    def q1_late(p, e):
        return q1_copy(
            ((q_late_even, q_late_odd)[p], ((z + 1) % GUESTS) * NY + e, q1_late_sem.at[p]), e, at(home_row, ys[e]))

    for p in range(2):
        @pl.when(early & (odd == p))
        def _():
            for e in Y_ORDER + (0,) * (1 - p):
                q1_row(p, e).start()

        @pl.when(late & (odd == p))
        def _():
            for e in Y_ORDER + (0,):
                q1_late(p, e).start()

    for c in range(PARTS):
        k_copy(c).start()
    for c in range(PARTS):
        v_copy(c).start()
    for copy in w_copies:
        copy.start()

    small_copies[1].wait()
    st_copies = [
        remote_copy(st_all.at[0], st_all.at[d], st_send_sem.at[d], st_recv_sem.at[d], (inst, t_peer[d]))
        for d in T_ORDER
    ]

    @pl.when(early)
    def _():
        for copy in st_copies:
            copy.start()

    query = q_own[...]
    q_row_odd[0] = query

    def relay_copy(own, relay, d, p, send_sem, recv_sem):
        return remote_copy(own, relay[p].at[d], send_sem.at[d], recv_sem.at[p, d], (z_peer[d], odd_t))

    for copy in small_copies[2:]:
        copy.wait()
    table = tab_ref[...]
    holder = table >> 6
    row_id = lax.broadcasted_iota(jnp.int32, table.shape, 0)
    page_id = lax.broadcasted_iota(jnp.int32, table.shape, 1)
    lent = (table >= 0) & (holder != row_id)
    lent_code = jnp.where(lent, row_id * SLOTS + (SLOTS - 1) - page_id, -1)
    lent_holder = jnp.where(lent, holder, -1)
    guest_code = [jnp.max(jnp.where(holder == z_peer[d], lent_code, -1)) for d in range(NZ)]
    lender = [jnp.max(jnp.where(row_id == y_peer[e], lent_holder, -1)) for e in range(NY)]

    own_length = len_smem[0, inst]
    own_row = jnp.broadcast_to(tab_ref[pl.ds(inst, 1), :] - inst * SLOTS, (SLOTS, SLOTS))
    slot_id = lax.broadcasted_iota(jnp.int32, (SLOTS, SLOTS), 0)
    page_of = lax.broadcasted_iota(jnp.int32, (SLOTS, SLOTS), 1)
    counted = jnp.clip(own_length - page_of * PAGE, 0, PAGE).astype(F32)
    valid = jnp.sum(jnp.where(own_row == slot_id, counted, 0.0), axis=1, keepdims=True)
    token = lax.broadcasted_iota(jnp.int32, (SLOTS, PAGE), 1).astype(F32)
    bias_buf[...] = jnp.where(token < valid, 0.0, NEG)

    guest = guest_code[0] >> 6
    first_page = (SLOTS - 1) - (guest_code[0] & (SLOTS - 1))
    guest_row = jnp.maximum(guest, 0)
    guest_length = jnp.where(guest >= 0, len_smem[0, guest_row], 0)
    guest_pages = ((guest_length + PAGE - 1) // PAGE) // 4
    page_token = lax.broadcasted_iota(jnp.int32, (1, PAGE), 1)
    slots = []
    limits = []
    for i in range(LENT):
        page = jnp.minimum(first_page + i, SLOTS - 1)
        slots.append(jnp.clip(tab_smem[guest_row, page] - inst * SLOTS, 0, SLOTS - 1))
        limits.append(jnp.where(i < guest_pages, guest_length - page * PAGE, 0))

    def scores_chunk(c, top):
        for p in range(CHUNK):
            slot = c * CHUNK + p
            s = lax.dot_general(query, k_buf[slot], NT_DIMS, preferred_element_type=F32)
            s = s + bias_buf[pl.ds(slot, 1), :]
            s_buf[c, :, p * PAGE:(p + 1) * PAGE] = s
            top = jnp.maximum(top, jnp.maximum(s[:, :HD], s[:, HD:]))
        return top

    def values_chunk(c, carry):
        total, numerator = carry
        half = CHUNK // 2
        for h in range(2):
            s = s_buf[c, :, h * half * PAGE:(h + 1) * half * PAGE]
            w = jnp.exp2(s * LOG2E_SCALE - own_top)
            total = total + lanes_sum(w)
            v = v_buf[pl.ds(c * CHUNK + h * half, half)].reshape(half * PAGE, HD)
            numerator = numerator + jnp.dot(w.astype(BF16), v, preferred_element_type=F32)
        return total, numerator

    per_part = CHUNKS // PARTS
    top = jnp.full((ROWS, HD), NEG, F32)
    for c in range(PARTS):
        k_copy(c).wait()
        top = lax.fori_loop(c * per_part, (c + 1) * per_part, scores_chunk, top)
    own_top = jnp.max(top, axis=1, keepdims=True) * LOG2E_SCALE

    def push(p, d, sent, received, slot, send_sem, recv_sem):
        return remote_copy(
            sent.at[p, d], received.at[slot], send_sem.at[p, d], recv_sem.at[slot], (z_peer[d], even_t + p))

    def push_all(p, source, pick, sent, received, slot, send_sem, recv_sem):
        for d in Z_ORDER + (0,):
            picked = source[pick(guest_code[d] >> 6)]
            if p == 1 and d == 0:
                received[slot] = picked
            else:
                sent[p, d] = picked
                push(p, d, sent, received, slot, send_sem, recv_sem).start()

    def push_done(sent, received, slot, send_sem, recv_sem):
        for p in range(2):
            for d in Z_ORDER + (0,) * (1 - p):
                push(p, d, sent, received, slot, send_sem, recv_sem).wait_send()

    @pl.when(early_relay)
    def _():
        for p in (1, 0):
            for e in Y_ORDER + (0,) * (1 - p):
                q1_row(p, e).wait_recv()
        pl.semaphore_wait(ready_sem, 2 * (NZ - EARLY))
        for p in FIRST_ORDER:
            push_all(
                p, (q_row_even, q_row_odd)[p], lambda r: (y - r) & (NY - 1),
                q_send_first, q_recv_first, row, qa_send_sem, qa_recv_sem)

    carry = (jnp.zeros((ROWS, HD), F32), jnp.zeros((ROWS, HD), F32))
    for c in range(PARTS):
        v_copy(c).wait()
        carry = lax.fori_loop(c * per_part, (c + 1) * per_part, values_chunk, carry)
    total, own_out = carry
    own_total = jnp.sum(total, axis=1, keepdims=True)

    @pl.when(home_relay)
    def _():
        for p in (1, 0):
            for j in range(GUESTS):
                for e in Y_ORDER + (0,):
                    slot = j * NY + e
                    remote_copy(
                        q_own, (q_late_even, q_late_odd)[p].at[slot], q1_send_sem.at[e], q1_late_sem.at[p, slot],
                        (inst, odd_t)).wait_recv()
            push_all(
                p, (q_late_even, q_late_odd)[p], lambda r: (((r >> 2) + 1) % GUESTS) * NY + ((y - r) & (NY - 1)),
                q_send_second, q_recv_second, home_place, qb_send_sem, qb_recv_sem)

    @pl.when(early_relay & (z == 0))
    def _():
        for d in (2, 4, 6):
            pl.semaphore_signal(plane_sem, inc=1, device_id=(inst, t_peer[d]), device_id_type=MESH)
        pl.semaphore_wait(plane_sem, NT // 2 - 1)
        for zz in range(EARLY, NZ):
            for which in (even_t, odd_t):
                pl.semaphore_signal(go_sem, inc=1, device_id=(at(zz, y), which), device_id_type=MESH)

    lane = lax.broadcasted_iota(jnp.int32, (ROWS, HD), 1)
    half_rows = ROWS // 2

    def lent_result(guest_query):
        guest_top = jnp.full((ROWS, HD), NEG, F32)
        for i in range(LENT):
            s = lax.dot_general(guest_query, k_buf[slots[i]], NT_DIMS, preferred_element_type=F32)
            s = jnp.where(page_token < limits[i], s, NEG)
            guest_buf[:, i * PAGE:(i + 1) * PAGE] = s
            guest_top = jnp.maximum(guest_top, jnp.maximum(s[:, :HD], s[:, HD:]))
        guest_top = jnp.max(guest_top, axis=1, keepdims=True) * LOG2E_SCALE
        total = jnp.zeros((ROWS, HD), F32)
        guest_out = jnp.zeros((ROWS, HD), F32)
        for i in range(LENT):
            s = guest_buf[:, i * PAGE:(i + 1) * PAGE]
            w = jnp.exp2(s * LOG2E_SCALE - guest_top)
            total = total + lanes_sum(w)
            guest_out = guest_out + jnp.dot(w.astype(BF16), v_buf[slots[i]], preferred_element_type=F32)
        guest_total = jnp.sum(total, axis=1, keepdims=True)
        level = jnp.broadcast_to(guest_top + jnp.log2(guest_total), (ROWS, HD))
        high = level.astype(BF16).astype(F32)
        middle = (level - high).astype(BF16).astype(F32)
        low = level - high - middle
        place = lane & 63
        coded = jnp.where(place == 0, high, jnp.where(place == 1, middle, jnp.where(place == 2, low, 0.0)))
        coded = jnp.where(lane[:half_rows] < 64, coded[:half_rows], coded[half_rows:])
        return jnp.concatenate([guest_out / guest_total, coded], axis=0).astype(BF16)

    p_relay = (p_relay_even, p_relay_odd)

    def send_result(own, wanted):
        for d in Z_ORDER:
            for p in range(2):
                @pl.when(wanted((z + d) % NZ) & (odd == p))
                def _():
                    relay_copy(own, p_relay, d, p, p1_send_sem, p1_recv_sem).start()

        @pl.when(wanted(z) & is_even)
        def _():
            relay_copy(own, p_relay, 0, 0, p1_send_sem, p1_recv_sem).start()

    def wait_arrival(received, slot, recv_sem, source):
        @pl.when(jnp.logical_not(is_relay & (z == source)))
        def _():
            remote_copy(
                received.at[slot], received.at[slot], recv_sem.at[slot], recv_sem.at[slot], (inst, odd_t)
            ).wait_recv()

    guest_z = guest_row >> 2
    for zz in range(EARLY):
        wait_arrival(q_recv_first, zz, qa_recv_sem, zz)
    result = lent_result(q_recv_first[jnp.minimum(guest_z, EARLY - 1)])
    p_own_first[...] = result
    send_result(p_own_first, lambda zz: zz < EARLY)

    @pl.when(early)
    def _():
        p_relay_odd[0] = result

    for j in range(2):
        wait_arrival(q_recv_second, j, qb_recv_sem, HOMES[j])
    result = lent_result(q_recv_second[jnp.where(guest_z >= 5, 0, 1)])
    p_own_second[...] = result
    send_result(p_own_second, lambda zz: zz >= EARLY)

    @pl.when(late)
    def _():
        p_relay_odd[0] = result
        pl.semaphore_wait(go_sem, 1)
        for copy in st_copies:
            copy.start()

    def relayed(relay, source, sent, received, arrive_sem, send_sem, recv_sem):
        @pl.when(is_relay)
        def _():
            for p in (1, 0):
                for d in Z_ORDER + (0,) * (1 - p):
                    relay_copy(sent.at[p, 0], relay, d, p, arrive_sem.at[p], arrive_sem).wait_recv()
                for e in Y_ORDER + (0,):
                    picked = relay[p][source[e]]
                    if p == 1 and e == 0:
                        received[0] = picked
                    else:
                        sent[p, e] = picked
                        remote_copy(
                            sent.at[p, e], received.at[e], send_sem.at[p, e], recv_sem.at[e], (y_peer[e], even_t + p)
                        ).start()

    def relay_done(sent, received, send_sem, recv_sem):
        for p in range(2):
            for e in Y_ORDER + (0,) * (1 - p):
                remote_copy(
                    sent.at[p, e], received.at[e], send_sem.at[p, e], recv_sem.at[e], (y_peer[e], even_t + p)
                ).wait_send()

    def arrived(received, recv_sem):
        for e in Y_ORDER:
            remote_copy(
                received.at[e], received.at[e], recv_sem.at[e], recv_sem.at[e], (y_peer[e], odd_t)
            ).wait_recv()

        @pl.when(jnp.logical_not(is_relay))
        def _():
            remote_copy(
                received.at[0], received.at[0], recv_sem.at[0], recv_sem.at[0], (inst, odd_t)
            ).wait_recv()

    relayed(
        p_relay, [(z - (lender[e] >> 2)) & (NZ - 1) for e in range(NY)], p_send, p_recv,
        p1_recv_sem, p2_send_sem, p2_recv_sem)
    for copy in w_copies:
        copy.wait()
    for copy in st_copies:
        copy.wait_recv()
    row16 = lax.broadcasted_iota(jnp.int32, (16, HD), 0) // STEPS

    def project(d, acc):
        source = (tensor - d + NT) % NT
        for h in range(2):
            x = st_all[d, h * 16:(h + 1) * 16, :].astype(F32)
            left = jnp.concatenate([jnp.where(row16 == g, x, 0.0) for g in range(4)], axis=1).astype(BF16)
            weight = jnp.concatenate(
                [kw_buf[source, h * 512:(h + 1) * 512, :], vw_buf[source, h * 512:(h + 1) * 512, :]], axis=1)
            acc = acc + jnp.dot(left, weight, preferred_element_type=F32)
        return acc

    acc = lax.fori_loop(0, NT, project, jnp.zeros((16, 2 * HD), F32))
    acc = acc[:8] + acc[8:]
    acc = acc[:4] + acc[4:]
    padded = jnp.concatenate([acc, jnp.zeros((12, 2 * HD), F32)], axis=0).astype(BF16)
    new_keys = padded[:, :HD]
    new_values = padded[:, HD:]
    s = lax.dot_general(query, new_keys, NT_DIMS, preferred_element_type=F32)
    step = lax.broadcasted_iota(jnp.int32, (ROWS, 16), 0) % STEPS
    other = lax.broadcasted_iota(jnp.int32, (ROWS, 16), 1)
    s = jnp.where(other <= step, s * LOG2E_SCALE, NEG)
    merged_top = jnp.maximum(own_top, jnp.max(s, axis=1, keepdims=True))
    w = jnp.exp2(s - merged_top)
    kept = jnp.exp2(own_top - merged_top)
    merged_total = own_total * kept + jnp.sum(w, axis=1, keepdims=True)
    merged_out = own_out * kept + jnp.dot(w.astype(BF16), new_values, preferred_element_type=F32)

    arrived(p_recv, p2_recv_sem)
    lent_part = p_recv[(y - lender[0]) & (NY - 1)].astype(F32)
    coded = lent_part[ROWS:]
    lane16 = lane[:half_rows]
    level = jnp.concatenate([
        jnp.sum(jnp.where(lane16 < 64, coded, 0.0), axis=1, keepdims=True),
        jnp.sum(jnp.where(lane16 < 64, 0.0, coded), axis=1, keepdims=True)], axis=0)
    level = jnp.where(lender[0] >= 0, level, NEG)
    highest = jnp.maximum(merged_top, level)
    kept = jnp.exp2(merged_top - highest)
    added = jnp.exp2(level - highest)
    out_ref[...] = (merged_out * kept + lent_part[:ROWS] * added) / (merged_total * kept + added)

    for copy in st_copies:
        copy.wait_send()
    for e in range(1, NY):
        q1_row(0, e).wait_send()

    @pl.when(late | is_even)
    def _():
        q1_row(0, 0).wait_send()

    for d in Z_ORDER:
        relay_copy(p_own_first, p_relay, d, 0, p1_send_sem, p1_recv_sem).wait_send()

    @pl.when(is_even)
    def _():
        relay_copy(p_own_first, p_relay, 0, 0, p1_send_sem, p1_recv_sem).wait_send()

    @pl.when(early_relay)
    def _():
        push_done(q_send_first, q_recv_first, row, qa_send_sem, qa_recv_sem)

    @pl.when(home_relay)
    def _():
        push_done(q_send_second, q_recv_second, home_place, qb_send_sem, qb_recv_sem)

    @pl.when(is_relay)
    def _():
        relay_done(p_send, p_recv, p2_send_sem, p2_recv_sem)


def on_device(queries, new_states, key_weight, value_weight, key_pool, value_pool, lengths, page_table):
    hbm = pl.BlockSpec(memory_space=pltpu.HBM)
    dma = pltpu.SemaphoreType.DMA

    def rows_of(x):
        return jnp.transpose(x.reshape(STEPS, GROUP, HD), (1, 0, 2)).reshape(ROWS, HD)

    out = pl.pallas_call(
        kernel,
        out_shape=pltpu.VMEM((ROWS, HD), F32),
        in_specs=[hbm] * 8,
        out_specs=pl.BlockSpec(memory_space=pltpu.VMEM),
        scratch_shapes=[
            pltpu.SMEM((1, 32), jnp.int32),
            pltpu.SMEM((32, SLOTS), jnp.int32),
            pltpu.VMEM((32, SLOTS), jnp.int32),
            pltpu.VMEM((SLOTS, PAGE, HD), BF16),
            pltpu.VMEM((SLOTS, PAGE, HD), BF16),
            pltpu.VMEM((NT, GROUP * HD, HD), BF16),
            pltpu.VMEM((NT, GROUP * HD, HD), BF16),
            pltpu.VMEM((CHUNKS, ROWS, CHUNK * PAGE), F32),
            pltpu.VMEM((ROWS, LENT * PAGE), F32),
            pltpu.VMEM((SLOTS, PAGE), F32),
            pltpu.VMEM((NT, ROWS, HD), BF16),
            pltpu.VMEM((ROWS, HD), BF16),
            pltpu.VMEM((NY, ROWS, HD), BF16),
            pltpu.VMEM((NY, ROWS, HD), BF16),
            pltpu.VMEM((GUESTS * NY, ROWS, HD), BF16),
            pltpu.VMEM((GUESTS * NY, ROWS, HD), BF16),
            pltpu.VMEM((2, NZ, ROWS, HD), BF16),
            pltpu.VMEM((2, NZ, ROWS, HD), BF16),
            pltpu.VMEM((EARLY, ROWS, HD), BF16),
            pltpu.VMEM((2, ROWS, HD), BF16),
            pltpu.VMEM((ROWS + 16, HD), BF16),
            pltpu.VMEM((ROWS + 16, HD), BF16),
            pltpu.VMEM((NZ, ROWS + 16, HD), BF16),
            pltpu.VMEM((NZ, ROWS + 16, HD), BF16),
            pltpu.VMEM((2, NY, ROWS + 16, HD), BF16),
            pltpu.VMEM((NY, ROWS + 16, HD), BF16),
            dma((5,)), dma((PARTS,)), dma((PARTS,)), dma((2,)), dma((NT,)), dma((NT,)),
            pltpu.SemaphoreType.REGULAR, pltpu.SemaphoreType.REGULAR, pltpu.SemaphoreType.REGULAR,
            dma((NY,)), dma((2, NY)), dma((2, GUESTS * NY)),
            dma((2, NZ)), dma((EARLY,)), dma((2, NZ)), dma((2,)),
            dma((NZ,)), dma((2, NZ)), dma((2, NY)), dma((NY,)),
        ],
        compiler_params=pltpu.CompilerParams(
            collective_id=0, has_side_effects=True, vmem_limit_bytes=VMEM_BYTES),
    )(
        lengths.reshape(1, -1), page_table, rows_of(queries), rows_of(new_states),
        key_weight.reshape(NT, GROUP * HD, HD), value_weight.reshape(NT, GROUP * HD, HD),
        key_pool, value_pool,
    )
    return (
        jnp.transpose(out.reshape(GROUP, STEPS, HD), (1, 0, 2))
        .reshape(1, STEPS, GROUP * HD)
        .astype(BF16)
    )


def solution(mesh):
    placed = (
        P("inst", None, "tensor"),
        P("inst", None, "tensor"),
        P(None, "tensor"),
        P(None, "tensor"),
        P("inst", None, "tensor"),
        P("inst", None, "tensor"),
        P(),
        P(),
    )
    return jax.shard_map(
        on_device, mesh=mesh, in_specs=placed, out_specs=P("inst", None, "tensor"), check_vma=False
    )
```

time: 25.1 us -> 23.7 us (0.944)
  the two profiles are of different devices: /device:TPU:4 before, /device:TPU:1 now
where the time goes in v5:
time: 23.7 us; the launch traced here: 23.6 us
  Pallas kernels  23 us (97%)
  other arithmetic  0.6 us (3%)
    pallas_call x1, Pallas kernels, on_device(): pl.pallas_call(kernel, out_shape=pltpu.VMEM((ROWS, HD), F32), in_specs=[h...  23 us
    convert_element_type x1, other arithmetic, on_device(): return jnp.transpose(out.reshape(GROUP, STEPS, HD), (1, 0, 2)).reshape(1,...  0.6 us

profile of v5, /device:TPU:1, one launch (start us, length us, event | category | flops | bytes accessed | tf_op | source)
XLA Modules:
  0.0 23.6 jit_solution(16313085179100489060)
XLA Ops:
  0.0 23.0 %shard_map.82 = f32[32,128]{1,0:T(8,128)S(1)} custom-call(s32[1,32]{1,0:T(1,128)} %bitcast.22, s32[32,64]{1,0:T(8,128)} %tab_hbm.1, bf16[32,128]{1,0:T(8,128)(2,1)} %bitcast.20, bf16[32,128]{1,0:T(8,128)(2,1)} %bitcast.21, bf16[8,1024,128]{2,1,0:T(8,128)(2,1)} %bitcast.18, bf16[8,1024,128]{2,1,0:T(8,128)(2,1)} %bitcast.19, bf16[64,256,128]{2,1,0:T(8,128)(2,1)} %k_hbm.1, ...), custom_call_target="tpu_custom_call" | custom-call | tf_op jit(solution)/shard_map/pallas_call | solution.py:508
  23.0 0.6 %convert_element_type.20 = bf16[32,128]{1,0:T(8,128)(2,1)} convert(f32[32,128]{1,0:T(8,128)S(1)} %shard_map.82) | non-fusion elementwise | flops 4096 | bytes 24576 | tf_op jit(solution)/shard_map/convert_element_type | solution.py:556

commit v6 on v5

--- a/solution.py
+++ b/solution.py
@@ -1,3 +1,4 @@
+import functools
 import math
 
 import jax
@@ -24,7 +25,7 @@
 EARLY = 2
 HOMES = (0, 1)
 GUESTS = 3
-FIRST_ORDER = (0, 1)
+FIRST = 3
 NEG = -1e30
 VMEM_BYTES = 60 * 1024 * 1024
 Z_ORDER = (4, 3, 5, 2, 6, 1, 7)
@@ -53,10 +54,10 @@
     len_hbm, tab_hbm, q_hbm, st_hbm, kw_hbm, vw_hbm, k_hbm, v_hbm,
     out_ref,
     len_smem, tab_smem, tab_ref, k_buf, v_buf, kw_buf, vw_buf, s_buf, guest_buf, bias_buf, st_all,
-    q_own, q_row_even, q_row_odd, q_late_even, q_late_odd, q_send_first, q_send_second, q_recv_first, q_recv_second,
+    kt_buf, new_buf, own_buf, q_own, q_row_even, q_row_odd, q_mid_even, q_mid_odd, q_late_even, q_late_odd, q_send_first, q_send_second, q_recv_first, q_recv_second,
     p_own_first, p_own_second, p_relay_even, p_relay_odd, p_send, p_recv,
     small_sem, k_sem, v_sem, w_sem, st_send_sem, st_recv_sem, ready_sem, plane_sem, go_sem,
-    q1_send_sem, q1_row_sem, q1_late_sem, qa_send_sem, qa_recv_sem, qb_send_sem, qb_recv_sem,
+    q1_send_sem, q1_row_sem, q1_mid_sem, q1_late_sem, qa_send_sem, qa_recv_sem, qb_send_sem, qb_recv_sem,
     p1_send_sem, p1_recv_sem, p2_send_sem, p2_recv_sem,
 ):
     inst = lax.axis_index("inst")
@@ -90,6 +91,13 @@
     def greet(where, which):
         pl.semaphore_signal(barrier, inc=1, device_id=(where, which), device_id_type=MESH)
 
+    @pl.when(late)
+    def _():
+        pl.semaphore_wait(barrier, EARLY + NY - 1)
+        for c in range(EARLY):
+            pl.semaphore_signal(
+                ready_sem, inc=1, device_id=(at((z + c) % EARLY, y), odd_t), device_id_type=MESH)
+
     @pl.when(early_relay)
     def _():
         for zz in range(NZ - 1, EARLY - 1, -1):
@@ -107,6 +115,9 @@
     def _():
         for c in range(1, EARLY):
             greet(at((z + c) % EARLY, y), odd_t)
+
+    @pl.when(z == 0)
+    def _():
         for d in T_ORDER:
             greet(inst, t_peer[d])
 
@@ -115,6 +126,10 @@
         for e in Y_ORDER:
             greet(y_peer[e], even_t)
             greet(y_peer[e], odd_t)
+
+    @pl.when(early_relay & (z > 0))
+    def _():
+        greet(inst, even_t)
 
     small_copies = [
         pltpu.make_async_copy(q_hbm, q_own, small_sem.at[0]),
@@ -139,13 +154,10 @@
         pltpu.make_async_copy(vw_hbm, vw_buf, w_sem.at[1]),
     ]
 
-    pl.semaphore_wait(barrier, jnp.where(late, EARLY + NY - 1, jnp.where(is_relay, NY - 1 + 2 * (EARLY - 1) + NT - 1, NY + NT - 2)))
-
-    @pl.when(late)
-    def _():
-        for c in range(EARLY):
-            pl.semaphore_signal(
-                ready_sem, inc=1, device_id=(at((z + c) % EARLY, y), odd_t), device_id_type=MESH)
+    @pl.when(early)
+    def _():
+        pl.semaphore_wait(
+            barrier, NY - 1 + odd * 2 * (EARLY - 1) + jnp.where(z == 0, NT - 1, 1 - odd))
 
     small_copies[0].wait()
 
@@ -156,17 +168,30 @@
     def q1_row(p, e):
         return q1_copy(((q_row_even, q_row_odd)[p], e, q1_row_sem.at[p]), e, y_peer[e])
 
+    def q1_mid(p, e):
+        return q1_copy(((q_mid_even, q_mid_odd)[p], e, q1_mid_sem.at[p]), e, at(home_row, ys[e]))
+
     def q1_late(p, e):
         return q1_copy(
             ((q_late_even, q_late_odd)[p], ((z + 1) % GUESTS) * NY + e, q1_late_sem.at[p]), e, at(home_row, ys[e]))
 
+    @pl.when(z == 0)
+    def _():
+        q_mid_even[...] = jnp.zeros_like(q_mid_even)
+        q_mid_odd[...] = jnp.zeros_like(q_mid_odd)
+
     for p in range(2):
         @pl.when(early & (odd == p))
         def _():
             for e in Y_ORDER + (0,) * (1 - p):
                 q1_row(p, e).start()
 
-        @pl.when(late & (odd == p))
+        @pl.when((z == EARLY) & (odd == p))
+        def _():
+            for e in Y_ORDER + (0,):
+                q1_mid(p, e).start()
+
+        @pl.when((z > EARLY) & (odd == p))
         def _():
             for e in Y_ORDER + (0,):
                 q1_late(p, e).start()
@@ -175,8 +200,6 @@
         k_copy(c).start()
     for c in range(PARTS):
         v_copy(c).start()
-    for copy in w_copies:
-        copy.start()
 
     small_copies[1].wait()
     st_copies = [
@@ -184,7 +207,7 @@
         for d in T_ORDER
     ]
 
-    @pl.when(early)
+    @pl.when(z == 0)
     def _():
         for copy in st_copies:
             copy.start()
@@ -256,13 +279,20 @@
         top = lax.fori_loop(c * per_part, (c + 1) * per_part, scores_chunk, top)
     own_top = jnp.max(top, axis=1, keepdims=True) * LOG2E_SCALE
 
+    def pick_first(p, r):
+        e = (y - r) & (NY - 1)
+        return lax.select((r >> 2) == EARLY, (q_mid_even, q_mid_odd)[p][e], (q_row_even, q_row_odd)[p][e])
+
+    def pick_second(p, r):
+        return (q_late_even, q_late_odd)[p][(((r >> 2) + 1) % GUESTS) * NY + ((y - r) & (NY - 1))]
+
     def push(p, d, sent, received, slot, send_sem, recv_sem):
         return remote_copy(
             sent.at[p, d], received.at[slot], send_sem.at[p, d], recv_sem.at[slot], (z_peer[d], even_t + p))
 
-    def push_all(p, source, pick, sent, received, slot, send_sem, recv_sem):
+    def push_all(p, pick, sent, received, slot, send_sem, recv_sem):
         for d in Z_ORDER + (0,):
-            picked = source[pick(guest_code[d] >> 6)]
+            picked = pick(guest_code[d] >> 6)
             if p == 1 and d == 0:
                 received[slot] = picked
             else:
@@ -274,45 +304,63 @@
             for d in Z_ORDER + (0,) * (1 - p):
                 push(p, d, sent, received, slot, send_sem, recv_sem).wait_send()
 
+    for copy in w_copies:
+        copy.start()
+
     @pl.when(early_relay)
     def _():
         for p in (1, 0):
             for e in Y_ORDER + (0,) * (1 - p):
                 q1_row(p, e).wait_recv()
+
+        @pl.when(z == HOMES[1])
+        def _():
+            for p in (1, 0):
+                for e in Y_ORDER + (0,):
+                    q1_mid(p, e).wait_recv()
+
+        for p in range(2):
+            for d in range(NZ):
+                picked = pick_first(p, guest_code[d] >> 6)
+                if p == 1 and d == 0:
+                    q_recv_first[row] = picked
+                else:
+                    q_send_first[p, d] = picked
         pl.semaphore_wait(ready_sem, 2 * (NZ - EARLY))
-        for p in FIRST_ORDER:
-            push_all(
-                p, (q_row_even, q_row_odd)[p], lambda r: (y - r) & (NY - 1),
-                q_send_first, q_recv_first, row, qa_send_sem, qa_recv_sem)
-
-    carry = (jnp.zeros((ROWS, HD), F32), jnp.zeros((ROWS, HD), F32))
+        for d in Z_ORDER + (0,):
+            for p in range(2 if d else 1):
+                push(p, d, q_send_first, q_recv_first, row, qa_send_sem, qa_recv_sem).start()
+
+    @pl.when(early_relay & (z == 0))
+    def _():
+        for d in (2, 4, 6):
+            pl.semaphore_signal(plane_sem, inc=1, device_id=(inst, t_peer[d]), device_id_type=MESH)
+
+    def own_values():
+        total, numerator = lax.fori_loop(
+            0, CHUNKS, values_chunk, (jnp.zeros((ROWS, HD), F32), jnp.zeros((ROWS, HD), F32)))
+        own_buf[0] = total
+        own_buf[1] = numerator
+
     for c in range(PARTS):
         v_copy(c).wait()
-        carry = lax.fori_loop(c * per_part, (c + 1) * per_part, values_chunk, carry)
-    total, own_out = carry
-    own_total = jnp.sum(total, axis=1, keepdims=True)
+    pl.when(early)(own_values)
 
     @pl.when(home_relay)
     def _():
         for p in (1, 0):
             for j in range(GUESTS):
-                for e in Y_ORDER + (0,):
-                    slot = j * NY + e
-                    remote_copy(
-                        q_own, (q_late_even, q_late_odd)[p].at[slot], q1_send_sem.at[e], q1_late_sem.at[p, slot],
-                        (inst, odd_t)).wait_recv()
+                @pl.when((z == HOMES[0]) | (j > 0))
+                def _():
+                    for e in Y_ORDER + (0,):
+                        slot = j * NY + e
+                        remote_copy(
+                            q_own, (q_late_even, q_late_odd)[p].at[slot], q1_send_sem.at[e],
+                            q1_late_sem.at[p, slot], (inst, odd_t)).wait_recv()
+
             push_all(
-                p, (q_late_even, q_late_odd)[p], lambda r: (((r >> 2) + 1) % GUESTS) * NY + ((y - r) & (NY - 1)),
+                p, functools.partial(pick_second, p),
                 q_send_second, q_recv_second, home_place, qb_send_sem, qb_recv_sem)
-
-    @pl.when(early_relay & (z == 0))
-    def _():
-        for d in (2, 4, 6):
-            pl.semaphore_signal(plane_sem, inc=1, device_id=(inst, t_peer[d]), device_id_type=MESH)
-        pl.semaphore_wait(plane_sem, NT // 2 - 1)
-        for zz in range(EARLY, NZ):
-            for which in (even_t, odd_t):
-                pl.semaphore_signal(go_sem, inc=1, device_id=(at(zz, y), which), device_id_type=MESH)
 
     lane = lax.broadcasted_iota(jnp.int32, (ROWS, HD), 1)
     half_rows = ROWS // 2
@@ -320,7 +368,7 @@
     def lent_result(guest_query):
         guest_top = jnp.full((ROWS, HD), NEG, F32)
         for i in range(LENT):
-            s = lax.dot_general(guest_query, k_buf[slots[i]], NT_DIMS, preferred_element_type=F32)
+            s = jnp.dot(guest_query, kt_buf[:, i * PAGE:(i + 1) * PAGE], preferred_element_type=F32)
             s = jnp.where(page_token < limits[i], s, NEG)
             guest_buf[:, i * PAGE:(i + 1) * PAGE] = s
             guest_top = jnp.maximum(guest_top, jnp.maximum(s[:, :HD], s[:, HD:]))
@@ -344,16 +392,21 @@
 
     p_relay = (p_relay_even, p_relay_odd)
 
-    def send_result(own, wanted):
-        for d in Z_ORDER:
-            for p in range(2):
-                @pl.when(wanted((z + d) % NZ) & (odd == p))
-                def _():
-                    relay_copy(own, p_relay, d, p, p1_send_sem, p1_recv_sem).start()
-
-        @pl.when(wanted(z) & is_even)
-        def _():
-            relay_copy(own, p_relay, 0, 0, p1_send_sem, p1_recv_sem).start()
+    def result_copy(own, zz, p):
+        slot = (zz - z) & (NZ - 1)
+        return remote_copy(
+            own, p_relay[p].at[slot], p1_send_sem.at[zz], p1_recv_sem.at[p, slot], (at(zz, y), odd_t))
+
+    def send_result(own, rows):
+        @pl.when(is_even)
+        def _():
+            for zz in rows:
+                result_copy(own, zz, 0).start()
+
+        for zz in rows:
+            @pl.when(is_relay & (z != zz))
+            def _():
+                result_copy(own, zz, 1).start()
 
     def wait_arrival(received, slot, recv_sem, source):
         @pl.when(jnp.logical_not(is_relay & (z == source)))
@@ -363,28 +416,66 @@
             ).wait_recv()
 
     guest_z = guest_row >> 2
+    for i in range(LENT):
+        kt_buf[:, i * PAGE:(i + 1) * PAGE] = k_buf[slots[i]].T
+
+    @pl.when(early_relay & (z == 0))
+    def _():
+        pl.semaphore_wait(plane_sem, NT // 2 - 1)
+        for zz in range(1, NZ):
+            for which in (even_t, odd_t):
+                pl.semaphore_signal(go_sem, inc=1, device_id=(at(zz, y), which), device_id_type=MESH)
+
     for zz in range(EARLY):
         wait_arrival(q_recv_first, zz, qa_recv_sem, zz)
     result = lent_result(q_recv_first[jnp.minimum(guest_z, EARLY - 1)])
     p_own_first[...] = result
-    send_result(p_own_first, lambda zz: zz < EARLY)
-
-    @pl.when(early)
+    send_result(p_own_first, range(FIRST))
+
+    @pl.when(z < FIRST)
     def _():
         p_relay_odd[0] = result
 
+    pl.when(late)(own_values)
     for j in range(2):
         wait_arrival(q_recv_second, j, qb_recv_sem, HOMES[j])
     result = lent_result(q_recv_second[jnp.where(guest_z >= 5, 0, 1)])
     p_own_second[...] = result
-    send_result(p_own_second, lambda zz: zz >= EARLY)
-
-    @pl.when(late)
+    send_result(p_own_second, range(FIRST, NZ))
+
+    @pl.when(z >= FIRST)
     def _():
         p_relay_odd[0] = result
+
+    @pl.when(z > 0)
+    def _():
         pl.semaphore_wait(go_sem, 1)
         for copy in st_copies:
             copy.start()
+
+    def project_all():
+        for copy in w_copies:
+            copy.wait()
+        for copy in st_copies:
+            copy.wait_recv()
+        row16 = lax.broadcasted_iota(jnp.int32, (16, HD), 0) // STEPS
+
+        def project(d, acc):
+            source = (tensor - d + NT) % NT
+            for h in range(2):
+                x = st_all[d, h * 16:(h + 1) * 16, :].astype(F32)
+                left = jnp.concatenate([jnp.where(row16 == g, x, 0.0) for g in range(4)], axis=1).astype(BF16)
+                weight = jnp.concatenate(
+                    [kw_buf[source, h * 512:(h + 1) * 512, :], vw_buf[source, h * 512:(h + 1) * 512, :]], axis=1)
+                acc = acc + jnp.dot(left, weight, preferred_element_type=F32)
+            return acc
+
+        acc = lax.fori_loop(0, NT, project, jnp.zeros((16, 2 * HD), F32))
+        acc = acc[:8] + acc[8:]
+        acc = acc[:4] + acc[4:]
+        new_buf[...] = jnp.concatenate([acc, jnp.zeros((12, 2 * HD), F32)], axis=0).astype(BF16)
+
+    pl.when(z == 0)(project_all)
 
     def relayed(relay, source, sent, received, arrive_sem, send_sem, recv_sem):
         @pl.when(is_relay)
@@ -424,28 +515,11 @@
     relayed(
         p_relay, [(z - (lender[e] >> 2)) & (NZ - 1) for e in range(NY)], p_send, p_recv,
         p1_recv_sem, p2_send_sem, p2_recv_sem)
-    for copy in w_copies:
-        copy.wait()
-    for copy in st_copies:
-        copy.wait_recv()
-    row16 = lax.broadcasted_iota(jnp.int32, (16, HD), 0) // STEPS
-
-    def project(d, acc):
-        source = (tensor - d + NT) % NT
-        for h in range(2):
-            x = st_all[d, h * 16:(h + 1) * 16, :].astype(F32)
-            left = jnp.concatenate([jnp.where(row16 == g, x, 0.0) for g in range(4)], axis=1).astype(BF16)
-            weight = jnp.concatenate(
-                [kw_buf[source, h * 512:(h + 1) * 512, :], vw_buf[source, h * 512:(h + 1) * 512, :]], axis=1)
-            acc = acc + jnp.dot(left, weight, preferred_element_type=F32)
-        return acc
-
-    acc = lax.fori_loop(0, NT, project, jnp.zeros((16, 2 * HD), F32))
-    acc = acc[:8] + acc[8:]
-    acc = acc[:4] + acc[4:]
-    padded = jnp.concatenate([acc, jnp.zeros((12, 2 * HD), F32)], axis=0).astype(BF16)
-    new_keys = padded[:, :HD]
-    new_values = padded[:, HD:]
+    pl.when(z > 0)(project_all)
+    own_total = jnp.sum(own_buf[0], axis=1, keepdims=True)
+    own_out = own_buf[1]
+    new_keys = new_buf[:, :HD]
+    new_values = new_buf[:, HD:]
     s = lax.dot_general(query, new_keys, NT_DIMS, preferred_element_type=F32)
     step = lax.broadcasted_iota(jnp.int32, (ROWS, 16), 0) % STEPS
     other = lax.broadcasted_iota(jnp.int32, (ROWS, 16), 1)
@@ -478,12 +552,10 @@
     def _():
         q1_row(0, 0).wait_send()
 
-    for d in Z_ORDER:
-        relay_copy(p_own_first, p_relay, d, 0, p1_send_sem, p1_recv_sem).wait_send()
-
-    @pl.when(is_even)
-    def _():
-        relay_copy(p_own_first, p_relay, 0, 0, p1_send_sem, p1_recv_sem).wait_send()
+    for zz in range(NZ):
+        @pl.when(is_even | (z != zz))
+        def _():
+            result_copy(p_own_first, zz, 0).wait_send()
 
     @pl.when(early_relay)
     def _():
@@ -522,7 +594,12 @@
             pltpu.VMEM((ROWS, LENT * PAGE), F32),
             pltpu.VMEM((SLOTS, PAGE), F32),
             pltpu.VMEM((NT, ROWS, HD), BF16),
+            pltpu.VMEM((HD, LENT * PAGE), BF16),
+            pltpu.VMEM((16, 2 * HD), BF16),
+            pltpu.VMEM((2, ROWS, HD), F32),
             pltpu.VMEM((ROWS, HD), BF16),
+            pltpu.VMEM((NY, ROWS, HD), BF16),
+            pltpu.VMEM((NY, ROWS, HD), BF16),
             pltpu.VMEM((NY, ROWS, HD), BF16),
             pltpu.VMEM((NY, ROWS, HD), BF16),
             pltpu.VMEM((GUESTS * NY, ROWS, HD), BF16),
@@ -539,7 +616,7 @@
             pltpu.VMEM((NY, ROWS + 16, HD), BF16),
             dma((5,)), dma((PARTS,)), dma((PARTS,)), dma((2,)), dma((NT,)), dma((NT,)),
             pltpu.SemaphoreType.REGULAR, pltpu.SemaphoreType.REGULAR, pltpu.SemaphoreType.REGULAR,
-            dma((NY,)), dma((2, NY)), dma((2, GUESTS * NY)),
+            dma((NY,)), dma((2, NY)), dma((2, NY)), dma((2, GUESTS * NY)),
             dma((2, NZ)), dma((EARLY,)), dma((2, NZ)), dma((2,)),
             dma((NZ,)), dma((2, NZ)), dma((2, NY)), dma((NY,)),
         ],

time: 23.7 us -> 23.1 us (0.975)
  the two profiles are of different devices: /device:TPU:1 before, /device:TPU:4 now
where the time goes in v6:
time: 23.1 us; the launch traced here: 22.8 us
  Pallas kernels  22.2 us (96%)
  other arithmetic  0.6 us (3%)
    pallas_call x1, Pallas kernels, on_device(): pl.pallas_call(kernel, out_shape=pltpu.VMEM((ROWS, HD), F32), in_specs=[h...  22.2 us
    convert_element_type x1, other arithmetic, on_device(): return jnp.transpose(out.reshape(GROUP, STEPS, HD), (1, 0, 2)).reshape(1,...  0.6 us

profile of v6, /device:TPU:4, one launch (start us, length us, event | category | flops | bytes accessed | tf_op | source)
XLA Modules:
  0.0 22.8 jit_solution(564790476924271819)
XLA Ops:
  0.0 22.2 %shard_map.82 = f32[32,128]{1,0:T(8,128)S(1)} custom-call(s32[1,32]{1,0:T(1,128)} %bitcast.22, s32[32,64]{1,0:T(8,128)} %tab_hbm.1, bf16[32,128]{1,0:T(8,128)(2,1)} %bitcast.20, bf16[32,128]{1,0:T(8,128)(2,1)} %bitcast.21, bf16[8,1024,128]{2,1,0:T(8,128)(2,1)} %bitcast.18, bf16[8,1024,128]{2,1,0:T(8,128)(2,1)} %bitcast.19, bf16[64,256,128]{2,1,0:T(8,128)(2,1)} %k_hbm.1, ...), custom_call_target="tpu_custom_call" | custom-call | tf_op jit(solution)/shard_map/pallas_call | solution.py:580
  22.2 0.6 %convert_element_type.20 = bf16[32,128]{1,0:T(8,128)(2,1)} convert(f32[32,128]{1,0:T(8,128)S(1)} %shard_map.82) | non-fusion elementwise | flops 4096 | bytes 24576 | tf_op jit(solution)/shard_map/convert_element_type | solution.py:633

commit v7 on v6

--- a/solution.py
+++ b/solution.py
@@ -54,7 +54,7 @@
     len_hbm, tab_hbm, q_hbm, st_hbm, kw_hbm, vw_hbm, k_hbm, v_hbm,
     out_ref,
     len_smem, tab_smem, tab_ref, k_buf, v_buf, kw_buf, vw_buf, s_buf, guest_buf, bias_buf, st_all,
-    kt_buf, new_buf, own_buf, q_own, q_row_even, q_row_odd, q_mid_even, q_mid_odd, q_late_even, q_late_odd, q_send_first, q_send_second, q_recv_first, q_recv_second,
+    kt_buf, vl_buf, lent_bias, new_buf, own_buf, q_own, q_row_even, q_row_odd, q_mid_even, q_mid_odd, q_late_even, q_late_odd, q_send_first, q_send_second, q_recv_first, q_recv_second,
     p_own_first, p_own_second, p_relay_even, p_relay_odd, p_send, p_recv,
     small_sem, k_sem, v_sem, w_sem, st_send_sem, st_recv_sem, ready_sem, plane_sem, go_sem,
     q1_send_sem, q1_row_sem, q1_mid_sem, q1_late_sem, qa_send_sem, qa_recv_sem, qb_send_sem, qb_recv_sem,
@@ -96,7 +96,7 @@
         pl.semaphore_wait(barrier, EARLY + NY - 1)
         for c in range(EARLY):
             pl.semaphore_signal(
-                ready_sem, inc=1, device_id=(at((z + c) % EARLY, y), odd_t), device_id_type=MESH)
+                ready_sem.at[odd], inc=1, device_id=(at((z + c) % EARLY, y), odd_t), device_id_type=MESH)
 
     @pl.when(early_relay)
     def _():
@@ -326,9 +326,9 @@
                     q_recv_first[row] = picked
                 else:
                     q_send_first[p, d] = picked
-        pl.semaphore_wait(ready_sem, 2 * (NZ - EARLY))
-        for d in Z_ORDER + (0,):
-            for p in range(2 if d else 1):
+        for p in (1, 0):
+            pl.semaphore_wait(ready_sem.at[p], NZ - EARLY)
+            for d in Z_ORDER + (0,) * (1 - p):
                 push(p, d, q_send_first, q_recv_first, row, qa_send_sem, qa_recv_sem).start()
 
     @pl.when(early_relay & (z == 0))
@@ -366,20 +366,25 @@
     half_rows = ROWS // 2
 
     def lent_result(guest_query):
-        guest_top = jnp.full((ROWS, HD), NEG, F32)
+        tops = []
         for i in range(LENT):
             s = jnp.dot(guest_query, kt_buf[:, i * PAGE:(i + 1) * PAGE], preferred_element_type=F32)
-            s = jnp.where(page_token < limits[i], s, NEG)
+            s = s + lent_bias[i:i + 1, :]
             guest_buf[:, i * PAGE:(i + 1) * PAGE] = s
-            guest_top = jnp.maximum(guest_top, jnp.maximum(s[:, :HD], s[:, HD:]))
-        guest_top = jnp.max(guest_top, axis=1, keepdims=True) * LOG2E_SCALE
-        total = jnp.zeros((ROWS, HD), F32)
+            tops.append(jnp.maximum(s[:, :HD], s[:, HD:]))
+        while len(tops) > 1:
+            tops = [jnp.maximum(m, n) for m, n in zip(tops[::2], tops[1::2])]
+        guest_top = jnp.max(tops[0], axis=1, keepdims=True) * LOG2E_SCALE
+        totals = []
         guest_out = jnp.zeros((ROWS, HD), F32)
-        for i in range(LENT):
-            s = guest_buf[:, i * PAGE:(i + 1) * PAGE]
+        wide = 4 * PAGE
+        for i in range(LENT // 4):
+            s = guest_buf[:, i * wide:(i + 1) * wide]
             w = jnp.exp2(s * LOG2E_SCALE - guest_top)
-            total = total + lanes_sum(w)
-            guest_out = guest_out + jnp.dot(w.astype(BF16), v_buf[slots[i]], preferred_element_type=F32)
+            totals.append(lanes_sum(w))
+            guest_out = guest_out + jnp.dot(
+                w.astype(BF16), vl_buf[i * wide:(i + 1) * wide, :], preferred_element_type=F32)
+        total = (totals[0] + totals[1]) + (totals[2] + totals[3])
         guest_total = jnp.sum(total, axis=1, keepdims=True)
         level = jnp.broadcast_to(guest_top + jnp.log2(guest_total), (ROWS, HD))
         high = level.astype(BF16).astype(F32)
@@ -418,6 +423,8 @@
     guest_z = guest_row >> 2
     for i in range(LENT):
         kt_buf[:, i * PAGE:(i + 1) * PAGE] = k_buf[slots[i]].T
+        vl_buf[i * PAGE:(i + 1) * PAGE, :] = v_buf[slots[i]]
+        lent_bias[i:i + 1, :] = jnp.where(page_token < limits[i], 0.0, NEG)
 
     @pl.when(early_relay & (z == 0))
     def _():
@@ -595,6 +602,8 @@
             pltpu.VMEM((SLOTS, PAGE), F32),
             pltpu.VMEM((NT, ROWS, HD), BF16),
             pltpu.VMEM((HD, LENT * PAGE), BF16),
+            pltpu.VMEM((LENT * PAGE, HD), BF16),
+            pltpu.VMEM((LENT, PAGE), F32),
             pltpu.VMEM((16, 2 * HD), BF16),
             pltpu.VMEM((2, ROWS, HD), F32),
             pltpu.VMEM((ROWS, HD), BF16),
@@ -615,7 +624,7 @@
             pltpu.VMEM((2, NY, ROWS + 16, HD), BF16),
             pltpu.VMEM((NY, ROWS + 16, HD), BF16),
             dma((5,)), dma((PARTS,)), dma((PARTS,)), dma((2,)), dma((NT,)), dma((NT,)),
-            pltpu.SemaphoreType.REGULAR, pltpu.SemaphoreType.REGULAR, pltpu.SemaphoreType.REGULAR,
+            pltpu.SemaphoreType.REGULAR((2,)), pltpu.SemaphoreType.REGULAR, pltpu.SemaphoreType.REGULAR,
             dma((NY,)), dma((2, NY)), dma((2, NY)), dma((2, GUESTS * NY)),
             dma((2, NZ)), dma((EARLY,)), dma((2, NZ)), dma((2,)),
             dma((NZ,)), dma((2, NZ)), dma((2, NY)), dma((NY,)),

time: 23.1 us -> 22.9 us (level)
  no operation moved by 1% of the time
where the time goes in v7:
time: 22.9 us; the launch traced here: 22.8 us
  Pallas kernels  22.2 us (97%)
  other arithmetic  0.6 us (3%)
    pallas_call x1, Pallas kernels, on_device(): pl.pallas_call(kernel, out_shape=pltpu.VMEM((ROWS, HD), F32), in_specs=[h...  22.2 us
    convert_element_type x1, other arithmetic, on_device(): return jnp.transpose(out.reshape(GROUP, STEPS, HD), (1, 0, 2)).reshape(1,...  0.6 us

profile of v7, /device:TPU:4, one launch (start us, length us, event | category | flops | bytes accessed | tf_op | source)
XLA Modules:
  0.0 22.8 jit_solution(1656323624449249257)
XLA Ops:
  0.0 22.2 %shard_map.82 = f32[32,128]{1,0:T(8,128)S(1)} custom-call(s32[1,32]{1,0:T(1,128)} %bitcast.22, s32[32,64]{1,0:T(8,128)} %tab_hbm.1, bf16[32,128]{1,0:T(8,128)(2,1)} %bitcast.20, bf16[32,128]{1,0:T(8,128)(2,1)} %bitcast.21, bf16[8,1024,128]{2,1,0:T(8,128)(2,1)} %bitcast.18, bf16[8,1024,128]{2,1,0:T(8,128)(2,1)} %bitcast.19, bf16[64,256,128]{2,1,0:T(8,128)(2,1)} %k_hbm.1, ...), custom_call_target="tpu_custom_call" | custom-call | tf_op jit(solution)/shard_map/pallas_call | solution.py:587
  22.2 0.6 %convert_element_type.20 = bf16[32,128]{1,0:T(8,128)(2,1)} convert(f32[32,128]{1,0:T(8,128)S(1)} %shard_map.82) | non-fusion elementwise | flops 4096 | bytes 24576 | tf_op jit(solution)/shard_map/convert_element_type | solution.py:642

commit v8 on v7

--- a/solution.py
+++ b/solution.py
@@ -544,11 +544,13 @@
     level = jnp.concatenate([
         jnp.sum(jnp.where(lane16 < 64, coded, 0.0), axis=1, keepdims=True),
         jnp.sum(jnp.where(lane16 < 64, 0.0, coded), axis=1, keepdims=True)], axis=0)
-    level = jnp.where(lender[0] >= 0, level, NEG)
+    has_lender = lender[0] >= 0
+    level = jnp.where(has_lender, level, NEG)
+    lent_out = jnp.where(has_lender, lent_part[:ROWS], 0.0)
     highest = jnp.maximum(merged_top, level)
     kept = jnp.exp2(merged_top - highest)
     added = jnp.exp2(level - highest)
-    out_ref[...] = (merged_out * kept + lent_part[:ROWS] * added) / (merged_total * kept + added)
+    out_ref[...] = (merged_out * kept + lent_out * added) / (merged_total * kept + added)
 
     for copy in st_copies:
         copy.wait_send()

time: 22.9 us -> 22.9 us (level)
  no operation moved by 1% of the time
where the time goes in v8:
time: 22.9 us; the launch traced here: 22.8 us
  Pallas kernels  22.1 us (97%)
  other arithmetic  0.6 us (3%)
    pallas_call x1, Pallas kernels, on_device(): pl.pallas_call(kernel, out_shape=pltpu.VMEM((ROWS, HD), F32), in_specs=[h...  22.1 us
    convert_element_type x1, other arithmetic, on_device(): return jnp.transpose(out.reshape(GROUP, STEPS, HD), (1, 0, 2)).reshape(1,...  0.6 us

profile of v8, /device:TPU:4, one launch (start us, length us, event | category | flops | bytes accessed | tf_op | source)
XLA Modules:
  0.0 22.8 jit_solution(1972427125234532866)
XLA Ops:
  0.0 22.1 %shard_map.82 = f32[32,128]{1,0:T(8,128)S(1)} custom-call(s32[1,32]{1,0:T(1,128)} %bitcast.22, s32[32,64]{1,0:T(8,128)} %tab_hbm.1, bf16[32,128]{1,0:T(8,128)(2,1)} %bitcast.20, bf16[32,128]{1,0:T(8,128)(2,1)} %bitcast.21, bf16[8,1024,128]{2,1,0:T(8,128)(2,1)} %bitcast.18, bf16[8,1024,128]{2,1,0:T(8,128)(2,1)} %bitcast.19, bf16[64,256,128]{2,1,0:T(8,128)(2,1)} %k_hbm.1, ...), custom_call_target="tpu_custom_call" | custom-call | tf_op jit(solution)/shard_map/pallas_call | solution.py:589
  22.2 0.6 %convert_element_type.20 = bf16[32,128]{1,0:T(8,128)(2,1)} convert(f32[32,128]{1,0:T(8,128)S(1)} %shard_map.82) | non-fusion elementwise | flops 4096 | bytes 24576 | tf_op jit(solution)/shard_map/convert_element_type | solution.py:644

commit v9 on v8

--- a/solution.py
+++ b/solution.py
@@ -326,10 +326,15 @@
                     q_recv_first[row] = picked
                 else:
                     q_send_first[p, d] = picked
-        for p in (1, 0):
-            pl.semaphore_wait(ready_sem.at[p], NZ - EARLY)
-            for d in Z_ORDER + (0,) * (1 - p):
-                push(p, d, q_send_first, q_recv_first, row, qa_send_sem, qa_recv_sem).start()
+        pl.semaphore_wait(ready_sem.at[1], NZ - EARLY)
+        for d in Z_ORDER[:3]:
+            push(1, d, q_send_first, q_recv_first, row, qa_send_sem, qa_recv_sem).start()
+        pl.semaphore_wait(ready_sem.at[0], NZ - EARLY)
+        for d in Z_ORDER:
+            push(0, d, q_send_first, q_recv_first, row, qa_send_sem, qa_recv_sem).start()
+            if d not in Z_ORDER[:3]:
+                push(1, d, q_send_first, q_recv_first, row, qa_send_sem, qa_recv_sem).start()
+        push(0, 0, q_send_first, q_recv_first, row, qa_send_sem, qa_recv_sem).start()
 
     @pl.when(early_relay & (z == 0))
     def _():

time: 22.9 us -> 22.9 us (level)
  no operation moved by 1% of the time
where the time goes in v9:
time: 22.9 us; the launch traced here: 22.7 us
  Pallas kernels  22.1 us (97%)
  other arithmetic  0.6 us (3%)
    pallas_call x1, Pallas kernels, on_device(): pl.pallas_call(kernel, out_shape=pltpu.VMEM((ROWS, HD), F32), in_specs=[h...  22.1 us
    convert_element_type x1, other arithmetic, on_device(): return jnp.transpose(out.reshape(GROUP, STEPS, HD), (1, 0, 2)).reshape(1,...  0.6 us

profile of v9, /device:TPU:4, one launch (start us, length us, event | category | flops | bytes accessed | tf_op | source)
XLA Modules:
  0.0 22.7 jit_solution(2455641838739875086)
XLA Ops:
  0.0 22.1 %shard_map.82 = f32[32,128]{1,0:T(8,128)S(1)} custom-call(s32[1,32]{1,0:T(1,128)} %bitcast.22, s32[32,64]{1,0:T(8,128)} %tab_hbm.1, bf16[32,128]{1,0:T(8,128)(2,1)} %bitcast.20, bf16[32,128]{1,0:T(8,128)(2,1)} %bitcast.21, bf16[8,1024,128]{2,1,0:T(8,128)(2,1)} %bitcast.18, bf16[8,1024,128]{2,1,0:T(8,128)(2,1)} %bitcast.19, bf16[64,256,128]{2,1,0:T(8,128)(2,1)} %k_hbm.1, ...), custom_call_target="tpu_custom_call" | custom-call | tf_op jit(solution)/shard_map/pallas_call | solution.py:594
  22.1 0.6 %convert_element_type.20 = bf16[32,128]{1,0:T(8,128)(2,1)} convert(f32[32,128]{1,0:T(8,128)S(1)} %shard_map.82) | non-fusion elementwise | flops 4096 | bytes 24576 | tf_op jit(solution)/shard_map/convert_element_type | solution.py:649

commit v10 on v8

--- a/solution.py
+++ b/solution.py
@@ -367,11 +367,12 @@
 
     def lent_result(guest_query):
         tops = []
-        for i in range(LENT):
-            s = jnp.dot(guest_query, kt_buf[:, i * PAGE:(i + 1) * PAGE], preferred_element_type=F32)
-            s = s + lent_bias[i:i + 1, :]
-            guest_buf[:, i * PAGE:(i + 1) * PAGE] = s
-            tops.append(jnp.maximum(s[:, :HD], s[:, HD:]))
+        span = 4 * PAGE
+        for i in range(LENT // 4):
+            s = jnp.dot(guest_query, kt_buf[:, i * span:(i + 1) * span], preferred_element_type=F32)
+            s = s + lent_bias[:, i * span:(i + 1) * span]
+            guest_buf[:, i * span:(i + 1) * span] = s
+            tops += [s[:, b * HD:(b + 1) * HD] for b in range(span // HD)]
         while len(tops) > 1:
             tops = [jnp.maximum(m, n) for m, n in zip(tops[::2], tops[1::2])]
         guest_top = jnp.max(tops[0], axis=1, keepdims=True) * LOG2E_SCALE
@@ -424,7 +425,7 @@
     for i in range(LENT):
         kt_buf[:, i * PAGE:(i + 1) * PAGE] = k_buf[slots[i]].T
         vl_buf[i * PAGE:(i + 1) * PAGE, :] = v_buf[slots[i]]
-        lent_bias[i:i + 1, :] = jnp.where(page_token < limits[i], 0.0, NEG)
+        lent_bias[:, i * PAGE:(i + 1) * PAGE] = jnp.where(page_token < limits[i], 0.0, NEG)
 
     @pl.when(early_relay & (z == 0))
     def _():
@@ -605,7 +606,7 @@
             pltpu.VMEM((NT, ROWS, HD), BF16),
             pltpu.VMEM((HD, LENT * PAGE), BF16),
             pltpu.VMEM((LENT * PAGE, HD), BF16),
-            pltpu.VMEM((LENT, PAGE), F32),
+            pltpu.VMEM((1, LENT * PAGE), F32),
             pltpu.VMEM((16, 2 * HD), BF16),
             pltpu.VMEM((2, ROWS, HD), F32),
             pltpu.VMEM((ROWS, HD), BF16),

time: 22.9 us -> 22.9 us (level)
  no operation moved by 1% of the time
where the time goes in v10:
time: 22.9 us; the launch traced here: 22.8 us
  Pallas kernels  22.2 us (97%)
  other arithmetic  0.6 us (3%)
    pallas_call x1, Pallas kernels, on_device(): pl.pallas_call(kernel, out_shape=pltpu.VMEM((ROWS, HD), F32), in_specs=[h...  22.2 us
    convert_element_type x1, other arithmetic, on_device(): return jnp.transpose(out.reshape(GROUP, STEPS, HD), (1, 0, 2)).reshape(1,...  0.6 us

profile of v10, /device:TPU:4, one launch (start us, length us, event | category | flops | bytes accessed | tf_op | source)
XLA Modules:
  0.0 22.8 jit_solution(13367631181022839901)
XLA Ops:
  0.0 22.2 %shard_map.82 = f32[32,128]{1,0:T(8,128)S(1)} custom-call(s32[1,32]{1,0:T(1,128)} %bitcast.22, s32[32,64]{1,0:T(8,128)} %tab_hbm.1, bf16[32,128]{1,0:T(8,128)(2,1)} %bitcast.20, bf16[32,128]{1,0:T(8,128)(2,1)} %bitcast.21, bf16[8,1024,128]{2,1,0:T(8,128)(2,1)} %bitcast.18, bf16[8,1024,128]{2,1,0:T(8,128)(2,1)} %bitcast.19, bf16[64,256,128]{2,1,0:T(8,128)(2,1)} %k_hbm.1, ...), custom_call_target="tpu_custom_call" | custom-call | tf_op jit(solution)/shard_map/pallas_call | solution.py:590
  22.2 0.6 %convert_element_type.20 = bf16[32,128]{1,0:T(8,128)(2,1)} convert(f32[32,128]{1,0:T(8,128)S(1)} %shard_map.82) | non-fusion elementwise | flops 4096 | bytes 24576 | tf_op jit(solution)/shard_map/convert_element_type | solution.py:645
